TPU v7x, 32 devices: a whole 2x2x4 slice. The times are simulated.
32 devices in a mesh: seq: 4 (over z), chan: 4 (over y, x), dp: 2 (over core).
Axes of the slice: x: 2, y: 2, z: 4, core: 2. Of those that a mesh axis runs over, the one named last changes fastest.
Arguments:
- mr_query: bfloat16 [2, 8192, 512], P('dp', 'chan', 'seq'), may hold values from -6 to 6
- mr_key: bfloat16 [2, 8192, 512], P('dp', 'chan', 'seq'), may hold values from -6 to 6
- mr_value: bfloat16 [2, 8192, 512], P('dp', 'chan', 'seq'), may hold values from -6 to 6
- li_key: bfloat16 [2, 8192, 512], P('dp', 'chan', 'seq'), may hold values from -6 to 6
- li_value: bfloat16 [2, 8192, 512], P('dp', 'chan', 'seq'), may hold values from -6 to 6
- grad_out: bfloat16 [2, 8192, 512], P('dp', 'chan', 'seq'), may hold values from -6 to 6
- mr_filter: bfloat16 [512, 128], P('chan'), may hold values from -0.5 to 0.5
- li_residue: float32 [512, 16], P('chan'), may hold values from -1.5 to 1.5
- li_rate: float32 [512, 16], P('chan'), may hold values from 1.953125e-05 to 0.05
Outputs:
- grad_mr_query: bfloat16 [2, 8192, 512], P('dp', 'chan', 'seq')
- grad_mr_key: bfloat16 [2, 8192, 512], P('dp', 'chan', 'seq')
- grad_mr_value: bfloat16 [2, 8192, 512], P('dp', 'chan', 'seq')
- grad_li_key: bfloat16 [2, 8192, 512], P('dp', 'chan', 'seq')
- grad_li_value: bfloat16 [2, 8192, 512], P('dp', 'chan', 'seq')
- grad_filter: float32 [512, 128], P('chan')
- grad_residue: float32 [512, 16], P('chan')
All inputs are finite; a program needn't handle non-finite values.
Results may differ from a plain program's by a relative error of at most 0.012.
Values may be sent and summed in bfloat16 or wider, within the bound.
No kernel may reach another device: no remote copies, remote signals or barrier semaphores. Data moves between devices by JAX's collectives and lax.ppermute only.
A program may use at most 128 MiB of HBM per device.

v0:
```python
import functools

import jax
import jax.numpy as jnp
from jax import lax
from jax.experimental import pallas as pl
from jax.experimental.pallas import tpu as pltpu
from jax.sharding import PartitionSpec as P

F32 = jnp.float32
BF16 = jnp.bfloat16
TILE = 128
LANES = 16
PACK = TILE // LANES
CHUNK = 32
STEPS = 4
PIECES = 8
VMEM_LIMIT = 24 * 1024 * 1024


def nn(lhs, rhs):
    return lax.dot_general(lhs, rhs, (((1,), (0,)), ((), ())), preferred_element_type=F32)


def nt(lhs, rhs):
    return lax.dot_general(lhs, rhs, (((1,), (1,)), ((), ())), preferred_element_type=F32)


def iotas():
    rows = lax.broadcasted_iota(jnp.int32, (TILE, TILE), 0)
    cols = lax.broadcasted_iota(jnp.int32, (TILE, TILE), 1)
    return rows, cols


def ones_where(mask):
    return jnp.where(mask, 1.0, 0.0).astype(BF16)


def column(turned, mask):
    wide = jnp.concatenate([turned] * PACK, axis=0)
    return jnp.sum(jnp.where(mask, wide, 0.0), axis=1, keepdims=True)


def squeeze_groups(wide, mask):
    kept = jnp.where(mask, wide, 0.0)
    total = kept[:LANES]
    for g in range(1, PACK):
        total = total + kept[g * LANES : (g + 1) * LANES]
    return total


def spread_groups(narrow, mask):
    return jnp.where(mask, jnp.concatenate([narrow] * PACK, axis=0), 0.0)


def circulant(row):
    base = jnp.broadcast_to(row, (LANES, TILE))
    base = pltpu.roll(base, 0, 1, stride=1, stride_axis=0).astype(BF16)
    return jnp.concatenate(
        [base] + [pltpu.roll(base, LANES * j, 1) for j in range(1, PACK)], axis=0
    )


def reversal():
    rows, cols = iotas()
    return ones_where((rows + cols) % TILE == 0)


def one_minus_exp(value):
    series = jnp.full_like(value, 1.0)
    for order in (7, 6, 5, 4, 3, 2):
        series = 1.0 - value * series / order
    return jnp.where(value < 0.125, value * series, 1.0 - jnp.exp(-value))


def chunk_mask(shape, bit):
    return (lax.broadcasted_iota(jnp.int32, shape, 1) // CHUNK) & bit == 0


def pair_chunks(turned):
    parts = [turned[CHUNK * j : CHUNK * (j + 1), :] for j in range(TILE // CHUNK)]
    for bit in (1, 2):
        keep = chunk_mask((CHUNK, TILE), bit)
        for j in range(len(parts)):
            if j & bit == 0:
                low, high = parts[j], parts[j + bit]
                parts[j] = jnp.where(keep, low, pltpu.roll(high, CHUNK * bit, 1))
                parts[j + bit] = jnp.where(keep, pltpu.roll(low, TILE - CHUNK * bit, 1), high)
    return parts


def windows(before, now):
    lanes = lax.broadcasted_iota(jnp.int32, now.shape, 1)
    none = jnp.zeros_like(now)
    first, second = [none if before is None else before], [now]
    for j in range(1, TILE // CHUNK):
        left = TILE - CHUNK * j
        moved = pltpu.roll(now, left, 1)
        older = none if before is None else pltpu.roll(before, left, 1)
        first.append(jnp.where(lanes < left, older, moved))
        second.append(moved)
    return jnp.concatenate(
        [jnp.concatenate(first, axis=0), jnp.concatenate(second, axis=0)], axis=1
    )


def beside(first, second):
    return jnp.concatenate([first, second], axis=1)


def above(*arrays):
    return jnp.concatenate(arrays, axis=0)


def apart(first, second):
    none = jnp.zeros_like(first)
    return above(beside(first, none), beside(none, second))


def lag_rows(chunks, shifted_rows, own_rows):
    wide = nn(above(*[chunks * own for own in own_rows]), shifted_rows)
    rows = lax.broadcasted_iota(jnp.int32, (2 * CHUNK, TILE), 0) % CHUNK
    lanes = lax.broadcasted_iota(jnp.int32, (2 * CHUNK, TILE), 1)
    sums = jnp.where(lanes + rows < CHUNK, wide[:, TILE:], wide[:, :TILE])
    parts = []
    for start in (0, CHUNK):
        part = pltpu.roll(sums[start : start + CHUNK], 0, 1, stride=1, stride_axis=0)
        parts.append(part[:8] + part[8:16] + part[16:24] + part[24:])
    return above(*parts).astype(BF16)


def now_and_before(now, before, rows, half):
    both = beside(now, before)
    pieces = []
    for g in range(0, PACK, 2):
        circs = beside(*[circulant(rows[h : h + 1, :]) for h in (g, g + 1)])
        w_now = circs * half
        wide = nn(both[g * LANES : (g + 2) * LANES, :], above(w_now, circs - w_now))
        pieces += [wide[:LANES, :TILE], wide[LANES:, TILE:]]
    return jnp.concatenate(pieces, axis=0)


def within_shard(array, rows, half):
    pieces = []
    for g in range(0, PACK, 4):
        weights = [
            beside(*[circulant(rows[h : h + 1, :]) for h in (k, k + 1)]) * half
            for k in (g, g + 2)
        ]
        parts = [array[k * LANES : (k + 2) * LANES, :] for k in (g, g + 2)]
        wide = nn(apart(*parts), above(*weights))
        for k in range(4):
            column_at = (k % 2) * TILE
            pieces.append(wide[k * LANES : (k + 1) * LANES, column_at : column_at + TILE])
    return jnp.concatenate(pieces, axis=0)


def block_groups(at, blocks, block):
    rows, cols = iotas()
    return cols == rows // LANES + (at * blocks + block) * PACK


def gate_kernel(query, key, product, held, made, arrived, left):
    size = held.shape[1] // PIECES

    def fetch(array, step):
        span = pl.ds(step * size, size)
        return pltpu.make_async_copy(
            (query, key)[array].at[span, :], held.at[array, span, :], arrived.at[array, step]
        )

    def store(step):
        span = pl.ds(step * size, size)
        return pltpu.make_async_copy(made.at[span, :], product.at[span, :], left.at[step])

    for step in range(PIECES):
        for array in range(2):
            fetch(array, step).start()
    for step in range(PIECES):
        for array in range(2):
            fetch(array, step).wait()
        span = pl.ds(step * size, size)
        made[span, :] = held[0, span, :] * held[1, span, :]
        store(step).start()
    for step in range(PIECES):
        store(step).wait()


def state_kernel(grad, value, rate, state):
    rows, cols = iotas()
    offsets = cols.astype(F32)
    mask = rows // LANES == cols // LANES
    at = pl.program_id(0)
    blocks = state.shape[0]
    for block in range(blocks):
        span = pl.ds(block * TILE, TILE)
        rates = column(rate[...], block_groups(at, blocks, block))
        powers = jnp.exp(-rates * offsets).astype(BF16)
        dz2 = grad[span, :] * value[span, :]
        state[block] = squeeze_groups(nt(powers, dz2), mask).astype(BF16)


def spans(array):
    return [pl.ds(block * TILE, TILE) for block in range(array.shape[0] // TILE)]


def group_rows(table, block):
    return table[pl.ds(block * PACK, PACK), :]


def local_kernel(grad, value, rate, residue, du2, to_next, taps, wide_rate):
    rows, cols = iotas()
    mask = rows // LANES == cols // LANES
    offsets = cols.astype(F32)
    at = pl.program_id(0)
    blocks = wide_rate.shape[0]
    coeffs = residue[...] * jnp.sqrt(one_minus_exp(2.0 * rate[...]))
    owns = [block_groups(at, blocks, block) for block in range(blocks)]
    rates = [column(rate[...], own) for own in owns]
    scales = [column(coeffs, own) for own in owns]
    sums = [
        jnp.sum((jnp.exp(-each * offsets) * scale).reshape(PACK, LANES, TILE), axis=1)
        for each, scale in zip(rates, scales)
    ]
    taps[...] = above(*sums)
    turned = nn(above(*sums).astype(BF16), reversal())
    lower = ones_where(rows >= cols)
    lower_half = beside(lower, lower)
    for block, span in enumerate(spans(grad)):
        wide_rate[block] = squeeze_groups(jnp.broadcast_to(rates[block], (TILE, TILE)), mask)
        ends = jnp.exp(-rates[block] * (TILE - 1 - offsets))
        to_next[span, :] = (ends * scales[block]).astype(BF16)
    results = [
        within_shard(
            grad[span, :] * value[span, :], turned[block * PACK : (block + 1) * PACK], lower_half
        )
        for block, span in enumerate(spans(grad))
    ]
    for span, result in zip(spans(grad), results):
        du2[span, :] = result


def table_kernel(rate, dz1, to_end, power):
    _, cols = iotas()
    offsets = cols.astype(F32)
    lags = ((CHUNK - 1 - cols) % TILE).astype(F32)
    at = pl.program_id(0)
    blocks = power.shape[0] // TILE
    for block, span in enumerate(spans(power)):
        rates = column(rate[...], block_groups(at, blocks, block))
        power[span, :] = jnp.exp(-rates * lags).astype(BF16)
        to_end[span, :] = jnp.exp(-rates * (TILE - 1 - offsets)).astype(BF16)


def middle_kernel(states, local, to_next, li_key, value, dz1, du2):
    rows, cols = iotas()
    mask = rows // LANES == cols // LANES
    wides = [spread_groups(states[block], mask).T.astype(BF16) for block in range(states.shape[0])]
    totals = [
        local[span, :] + nn(wide, to_next[span, :]) for span, wide in zip(spans(local), wides)
    ]
    for span, total in zip(spans(local), totals):
        du2[span, :] = total
        dy1 = total * li_key[span, :].astype(F32)
        dz1[span, :] = (dy1 * value[span, :].astype(F32)).astype(BF16)


def forward_kernel(
    before, now, filters, value, li_key, to_end, dz1, grad, li_value, power, after_shard, rate,
    z1, u2, packed, filter_sums, within_sums, across_sums,
):
    rows, cols = iotas()
    mask = rows // LANES == cols // LANES
    upper = ones_where(cols >= rows)
    upper_half = beside(upper, upper)
    turn = ones_where(cols == rows - rows % CHUNK + (CHUNK - 1 - rows % CHUNK))
    lanes = lax.broadcasted_iota(jnp.int32, (CHUNK, TILE), 1)
    own_rows = [ones_where((lanes // LANES) % 2 == i) for i in range(2)]
    eights = ones_where(
        lax.broadcasted_iota(jnp.int32, (2 * PACK, TILE), 1) // 8
        == lax.broadcasted_iota(jnp.int32, (2 * PACK, TILE), 0)
    )
    at = pl.program_id(0)
    blocks = now.shape[0] // TILE

    @pl.when(at == 0)
    def _():
        within_sums[...] = jnp.zeros_like(within_sums)
        across_sums[...] = jnp.zeros_like(across_sums)

    turned = []
    for span in spans(now):
        dz2 = grad[span, :] * li_value[span, :]
        turned.append(nt(turn, above(dz1[span, :], dz2)).astype(BF16))
    chunks = [(pair_chunks(each[:, :TILE]), pair_chunks(each[:, TILE:])) for each in turned]
    results = [
        now_and_before(
            now[span, :], before[span, :], group_rows(filters, block).astype(F32), upper_half
        )
        for block, span in enumerate(spans(now))
    ]
    halves = []
    for span, result in zip(spans(now), results):
        z1[span, :] = result
        y1 = (value[span, :].astype(F32) * result).astype(BF16).astype(F32)
        halves.append((y1 * li_key[span, :].astype(F32)).astype(BF16))
        u2[span, :] = halves[-1]
    ends = [nt(to_end[span, :], half) for span, half in zip(spans(now), halves)]

    lags = []
    for block in range(blocks):
        lag, energy = [], []
        for p in range(TILE // CHUNK):
            pair = pl.ds(block * TILE + p * CHUNK, CHUNK)
            older, newer = before[pair, :], now[pair, :]
            later = halves[block][p * CHUNK : (p + 1) * CHUNK]
            lag.append(lag_rows(chunks[block][0][p], windows(older, newer), own_rows))
            energy.append(lag_rows(chunks[block][1][p], windows(None, later), own_rows))
        lags.append(above(*lag, *energy))
    lags = [nn(eights, each) for each in lags]
    within, across = jnp.zeros((LANES, TILE), F32), jnp.zeros((LANES, TILE), F32)
    for block, span in enumerate(spans(now)):
        own = block_groups(at, blocks, block)
        energies = above(*[lags[block][PACK:].astype(BF16)] * LANES)
        within = within + squeeze_groups(nt(power[span, :], energies), own)
        state = squeeze_groups(ends[block], mask).astype(BF16)
        crossing = state.astype(F32) * after_shard[block]
        across = across + nn(crossing.astype(BF16), ones_where(own))
        packed[at * blocks + block] = state
    lags = [each[:PACK] for each in lags]
    few = blocks * PACK
    filter_sums[pl.ds(pl.multiple_of(at * few, few), few), :] = above(*lags)
    within_sums[...] += within
    across_sums[...] += across

    steps = filter_sums.shape[0] // few

    @pl.when(at == steps - 1)
    def _():
        place = ones_where((rows + cols) % TILE == CHUNK - 1)
        sums = nn(filter_sums[...].astype(BF16), place).astype(BF16)
        for chunk in range(filter_sums.shape[0] // LANES):
            packed[steps * blocks + chunk] = sums[chunk * LANES : (chunk + 1) * LANES]
        gains = jnp.sqrt(one_minus_exp(2.0 * rate[...]))
        total = gains * (within_sums[...] + across_sums[...])
        packed[steps * blocks + filter_sums.shape[0] // LANES] = total.astype(BF16)


def factor_kernel(
    bits, wide_rate, rate, residue, filters, later, zeros, after, mr_turned, *weights
):
    zeros[...] = jnp.zeros_like(zeros)
    place = lax.axis_index("seq")
    rates = wide_rate[...]
    weights = list(weights)
    for bit in bits:
        high = (place & bit) != 0
        passed = TILE * (place & (bit - 1)) + 1
        reach = jnp.exp(-rates * passed.astype(F32))
        weights.pop(0)[...] = jnp.where(high, reach, 0.0)
        if bit != bits[-1]:
            run = jnp.exp(-rates * (TILE * bit))
            one = jnp.ones_like(run)
            weights.pop(0)[...] = jnp.where(high, run, one)
            weights.pop(0)[...] = jnp.where(high, one, run)
    mr_turned[...] = nn(filters[...], reversal())
    _, cols = iotas()
    coeffs = residue[...] * jnp.sqrt(one_minus_exp(2.0 * rate[...]))
    for block, span in enumerate(spans(after)):
        own = block_groups(0, 0, block)
        powers = jnp.exp(-column(rate[...], own) * cols.astype(F32))
        after[span, :] = (powers * column(coeffs, own)).astype(BF16)


def within_kernel(u2, taps, z1, du2, value, li_key, z2, grad_value, grad_key, zeros):
    zeros[...] = jnp.zeros_like(zeros)
    rows, cols = iotas()
    upper = ones_where(cols >= rows)
    upper_half = beside(upper, upper)
    results = [
        within_shard(u2[span, :], group_rows(taps, block), upper_half)
        for block, span in enumerate(spans(u2))
    ]
    for span, result in zip(spans(u2), results):
        z2[span, :] = result
        z1_here, du2_here = z1[span, :], du2[span, :]
        y1 = (value[span, :].astype(F32) * z1_here).astype(BF16).astype(F32)
        grad_key[span, :] = (du2_here * y1).astype(BF16)
        grad_value[span, :] = (du2_here * li_key[span, :].astype(F32) * z1_here).astype(BF16)


def product_kernel(dz1, later, turned, query, key, grad_query, grad_key):
    rows, cols = iotas()
    lower = ones_where(rows >= cols)
    lower_half = beside(lower, lower)
    results = [
        now_and_before(
            dz1[span, :], later[span, :], group_rows(turned, block), lower_half
        )
        for block, span in enumerate(spans(dz1))
    ]
    for span, du1 in zip(spans(dz1), results):
        grad_query[span, :] = (du1 * key[span, :].astype(F32)).astype(BF16)
        grad_key[span, :] = (du1 * query[span, :].astype(F32)).astype(BF16)


def value_kernel(
    states, after, z2, grad, half, other, grad_value, grad_filter, grad_residue,
    made, filter_sum, residue_sum, left, done,
):
    rows, cols = iotas()
    mask = rows // LANES == cols // LANES
    at = pl.program_id(0)
    size = z2.shape[0]
    sums = [
        pltpu.make_async_copy(filter_sum, grad_filter, done.at[0]),
        pltpu.make_async_copy(residue_sum, grad_residue, done.at[1]),
    ]

    @pl.when(at == 0)
    def _():
        chunks = half.shape[0] - 1
        for chunk in range(chunks):
            both = half[chunk].astype(F32) + other[chunk].astype(F32)
            filter_sum[pl.ds(chunk * LANES, LANES), :] = both
        residue_sum[...] = half[chunks].astype(F32) + other[chunks].astype(F32)
        for copy in sums:
            copy.start()

    def store(step):
        span = pl.ds(pl.multiple_of(step * size, size), size)
        return pltpu.make_async_copy(made.at[span, :], grad_value.at[span, :], left.at[step])

    wides = [spread_groups(states[block], mask).T.astype(BF16) for block in range(states.shape[0])]
    totals = [z2[span, :] + nn(wide, after[span, :]) for span, wide in zip(spans(z2), wides)]
    for block, (span, total) in enumerate(zip(spans(z2), totals)):
        here = pl.ds(pl.multiple_of(at * size + block * TILE, TILE), TILE)
        made[here, :] = (grad[span, :].astype(F32) * total).astype(BF16)
    store(at).start()

    @pl.when(at == STEPS - 1)
    def _():
        for copy in sums:
            copy.wait()
        for step in range(STEPS):
            store(step).wait()


def shifted(value, axis, steps):
    count = lax.axis_size(axis)
    first, last = max(0, -steps), min(count, count - steps)
    return lax.ppermute(value, axis, [(source, source + steps) for source in range(first, last)])


def swapped(value, axis, bit):
    count = lax.axis_size(axis)
    return lax.ppermute(value, axis, [(source, source ^ bit) for source in range(count)])


def scan_bits():
    count, bit, bits = lax.axis_size("seq"), 1, []
    assert count & (count - 1) == 0
    while bit < count:
        bits.append(bit)
        bit *= 2
    return bits


def per_device(
    mr_query, mr_key, mr_value, li_key, li_value, grad_out, mr_filter, li_residue, li_rate
):
    query, key, value, key_two, value_two, grad = (
        array[0] for array in (mr_query, mr_key, mr_value, li_key, li_value, grad_out)
    )
    groups, filt_len = mr_filter.shape
    channels, seq_local = query.shape
    assert filt_len == TILE and seq_local == TILE and groups <= TILE
    assert channels == groups * LANES and li_rate.shape[1] == LANES
    rows = channels // STEPS
    few = groups // STEPS
    spare = ((0, 0), (0, TILE - groups))
    rate = jnp.pad(li_rate.T, spare)
    residue = jnp.pad(li_residue.T, spare)

    blocks = channels // TILE

    wide = pl.BlockSpec((rows, TILE), lambda i: (i, 0))
    table = pl.BlockSpec((few, TILE), lambda i: (i, 0))
    chunk = pl.BlockSpec((blocks // STEPS, LANES, TILE), lambda i: (i, 0, 0))
    modes = pl.BlockSpec((LANES, TILE), lambda i: (0, 0))
    distant = pl.BlockSpec(memory_space=pltpu.HBM)
    anywhere = pl.BlockSpec(memory_space=pl.ANY)
    wide_half = jax.ShapeDtypeStruct((channels, TILE), BF16)
    wide_full = jax.ShapeDtypeStruct((channels, TILE), F32)
    table_full = jax.ShapeDtypeStruct((groups, TILE), F32)
    chunk_half = jax.ShapeDtypeStruct((blocks, LANES, TILE), BF16)
    chunk_full = jax.ShapeDtypeStruct((blocks, LANES, TILE), F32)

    def call(kernel, name, in_specs, out_specs, out_shape, scratch=(), grid=STEPS, limit=VMEM_LIMIT, work=0):
        return pl.pallas_call(
            kernel,
            grid=(grid,),
            in_specs=in_specs,
            out_specs=out_specs,
            out_shape=out_shape,
            scratch_shapes=scratch,
            name=name,
            cost_estimate=pl.CostEstimate(
                flops=2 * work * channels * TILE * TILE, bytes_accessed=1, transcendentals=0
            ),
            compiler_params=pltpu.CompilerParams(vmem_limit_bytes=limit),
        )

    def whole(leaf):
        return pl.BlockSpec(leaf.shape, lambda i: (0,) * len(leaf.shape))

    def twice(spec):
        return pl.BlockSpec((2 * spec.block_shape[0],) + spec.block_shape[1:], spec.index_map)

    (product,) = call(
        gate_kernel, "gate", [distant] * 2, [distant], [wide_half],
        [
            pltpu.VMEM((2, channels, TILE), BF16), pltpu.VMEM((channels, TILE), BF16),
            pltpu.SemaphoreType.DMA((2, PIECES)), pltpu.SemaphoreType.DMA((PIECES,)),
        ],
        grid=1, limit=60 * 1024 * 1024,
    )(query, key)
    product_before = shifted(product, "seq", 1)

    (back,) = call(state_kernel, "state", [wide, wide, modes], [chunk], [chunk_half])(
        grad, value_two, rate
    )

    later_backs = [shifted(back, "seq", -gap) for gap in range(1, lax.axis_size("seq"))]
    du2_local, to_next, taps, wide_rate = call(
        local_kernel, "local", [wide, wide, modes, modes], [wide, wide, table, chunk],
        [wide_full, wide_half, table_full, chunk_full],
    )(grad, value_two, rate, residue)
    fade = jnp.exp(-TILE * wide_rate)
    after_shard = later_backs[-1].astype(F32)
    for other in later_backs[-2::-1]:
        after_shard = other.astype(F32) + fade * after_shard
    after_shard = after_shard * jnp.exp(-wide_rate)

    dz1, du2 = call(
        middle_kernel, "middle", [twice(chunk)] + [twice(wide)] * 4, [twice(wide)] * 2,
        [wide_half, wide_full], grid=STEPS // 2,
    )(after_shard, du2_local, to_next, key_two, value)
    dz1_later = shifted(dz1, "seq", -1)
    to_end, power = call(
        table_kernel, "table", [modes, anywhere], [wide, wide], [wide_half, wide_half]
    )(rate, dz1)

    filter_chunks = groups // LANES
    packed_shape = jax.ShapeDtypeStruct((blocks + filter_chunks + 1, LANES, TILE), BF16)
    z1, u2, packed = call(
        forward_kernel, "forward",
        [twice(spec) for spec in [wide, wide, table] + [wide] * 7 + [chunk]] + [modes],
        [twice(wide), twice(wide), whole(packed_shape)], [wide_full, wide_half, packed_shape],
        [pltpu.VMEM((groups, TILE), F32)] + [pltpu.VMEM((LANES, TILE), F32)] * 2,
        grid=STEPS // 2,
    )(
        product_before, product, mr_filter, value, key_two, to_end, dz1, grad, value_two, power,
        after_shard, rate,
    )

    bits = scan_bits()
    few_full = jax.ShapeDtypeStruct((filter_chunks + 1, LANES, TILE), F32)
    factors = 3 * len(bits) - 2
    z2, grad_mr_value, grad_li_key, within_zeros = call(
        within_kernel, "within",
        [wide, table, wide, wide, wide, wide], [wide] * 3 + [whole(few_full)],
        [wide_full, wide_half, wide_half, few_full],
    )(u2, taps, z1, du2, value, key_two)

    factor_shapes = [few_full, wide_half, table_full] + [chunk_full] * factors
    factor_zeros, after, mr_turned, *weights = call(
        functools.partial(factor_kernel, bits), "factor",
        [whole(chunk_full), modes, modes, whole(mr_filter), anywhere],
        [whole(leaf) for leaf in factor_shapes], factor_shapes, grid=1,
    )(wide_rate, rate, residue, mr_filter, dz1_later)

    grad_query, grad_key = call(
        product_kernel, "product",
        [twice(spec) for spec in (wide, wide, table, wide, wide)],
        [twice(wide), twice(wide)], [wide_half, wide_half], grid=STEPS // 2,
    )(dz1, dz1_later, mr_turned, query, key)

    assert lax.axis_size("dp") == 2
    half = packed[blocks:]
    sums = half.astype(F32) + swapped(half, "dp", 1).astype(F32) + within_zeros
    packed = jnp.concatenate([packed[:blocks], sums.astype(BF16)], axis=0)
    zeros = [factor_zeros]
    before_shard = jnp.zeros(back.shape, F32)
    for bit in bits:
        other = swapped(packed, "seq", bit)
        mine, theirs = packed[:blocks].astype(F32), other[:blocks].astype(F32)
        before_shard = before_shard + weights.pop(0) * theirs
        half, partner = packed[blocks:], other[blocks:]
        if bit != bits[-1]:
            sums = half.astype(F32) + partner.astype(F32)
            if zeros:
                sums = sums + zeros.pop(0)
            total = weights.pop(0) * theirs + weights.pop(0) * mine
            packed = jnp.concatenate([total.astype(BF16), sums.astype(BF16)], axis=0)
    residue_full = jax.ShapeDtypeStruct((LANES, TILE), F32)
    grad_li_value, grad_filter, grad_residue = call(
        value_kernel, "value",
        [chunk, wide, wide, wide, whole(half), whole(half)],
        [distant] * 3, [wide_half, table_full, residue_full],
        [
            pltpu.VMEM((channels, TILE), BF16), pltpu.VMEM((groups, TILE), F32),
            pltpu.VMEM((LANES, TILE), F32),
            pltpu.SemaphoreType.DMA((STEPS,)), pltpu.SemaphoreType.DMA((2,)),
        ],
    )(before_shard, after, z2, grad, half, partner)

    return (
        grad_query[None],
        grad_key[None],
        grad_mr_value[None],
        grad_li_key[None],
        grad_li_value[None],
        grad_filter,
        grad_residue[:, :groups].T,
    )


def solution(mesh):
    streams = (P("dp", "chan", "seq"),)
    tables = (P("chan", None),)
    return jax.shard_map(
        per_device,
        mesh=mesh,
        in_specs=streams * 6 + tables * 3,
        out_specs=streams * 5 + tables * 2,
        check_vma=False,
    )
```

profile of v0, /device:TPU:0, one launch (start us, length us, event | category | flops | bytes accessed | tf_op | source)
XLA Modules:
  0.0 49.3 jit_solution(14861510966919592084)
XLA Ops:
  0.6 0.0 copy-start
  0.6 0.0 copy-start.1
  0.7 0.0 copy-start.7
  0.7 2.2 %gate.1.now = bf16[2048,128]{1,0:T(8,128)(2,1)} custom-call(bf16[2048,128]{1,0:T(8,128)(2,1)} %bitcast.27, bf16[2048,128]{1,0:T(8,128)(2,1)} %bitcast.29), custom_call_target="tpu_custom_call" | custom-call | bytes 1 | tf_op jit(solution)/shard_map/gate/pallas_call | solution.py:520
  2.8 5.0 %collective-permute-start.4 = (bf16[2048,128]{1,0:T(8,128)(2,1)}, bf16[2048,128]{1,0:T(8,128)(2,1)S(1)}, u32[]{:S(2)}, u32[]{:S(2)}) collective-permute-start(bf16[2048,128]{1,0:T(8,128)(2,1)} %gate.1.now), channel_id=1, source_target_pairs={{0,8},{8,16},{16,24},{1,9},{9,17},{17,25},{2,10},{10,18},{18,26},{... | collective-permute-start | bytes 1572872 | tf_op jit(solution)/shard_map/ppermute | solution.py:452
  7.8 0.0 copy-done
  7.8 0.0 copy-done.1
  7.8 0.0 copy-done.7
  7.8 0.0 copy-start.9
  7.8 1.2 %state.1 = bf16[16,16,128]{2,1,0:T(8,128)(2,1)S(1)} custom-call(bf16[2048,128]{1,0:T(8,128)(2,1)S(1)} %bitcast.14, bf16[2048,128]{1,0:T(8,128)(2,1)S(1)} %bitcast.18, f32[16,128]{1,0:T(8,128)S(1)} %bitcast.31), custom_call_target="tpu_custom_call" | custom-call | bytes 1 | tf_op jit(solution)/shard_map/state/pallas_call | solution.py:530
  9.0 1.3 %collective-permute-start = (bf16[16,16,128]{2,1,0:T(8,128)(2,1)S(1)}, bf16[16,16,128]{2,1,0:T(8,128)(2,1)S(1)}, u32[]{:S(2)}, u32[]{:S(2)}) collective-permute-start(bf16[16,16,128]{2,1,0:T(8,128)(2,1)S(1)} %state.1), channel_id=1, source_target_pairs={{8,0},{16,8},{24,16},{9,1},{17,9},{25,17},{10,2},{18,10},{26,18},{... | collective-permute-start | bytes 196616 | tf_op jit(solution)/shard_map/ppermute | solution.py:452
  10.3 1.3 %collective-permute-start.1 = (bf16[16,16,128]{2,1,0:T(8,128)(2,1)S(1)}, bf16[16,16,128]{2,1,0:T(8,128)(2,1)S(1)}, u32[]{:S(2)}, u32[]{:S(2)}) collective-permute-start(bf16[16,16,128]{2,1,0:T(8,128)(2,1)S(1)} %state.1), channel_id=1, source_target_pairs={{16,0},{24,8},{17,1},{25,9},{18,2},{26,10},{19,3},{27,11},{20,4},{... | collective-permute-start | bytes 196616 | tf_op jit(solution)/shard_map/ppermute | solution.py:452
  11.6 1.3 %collective-permute-start.2 = (bf16[16,16,128]{2,1,0:T(8,128)(2,1)S(1)}, bf16[16,16,128]{2,1,0:T(8,128)(2,1)S(1)}, u32[]{:S(2)}, u32[]{:S(2)}) collective-permute-start(bf16[16,16,128]{2,1,0:T(8,128)(2,1)S(1)} %state.1), channel_id=1, source_target_pairs={{24,0},{25,1},{26,2},{27,3},{28,4},{29,5},{30,6},{31,7}} | collective-permute-start | bytes 196616 | tf_op jit(solution)/shard_map/ppermute | solution.py:452
  12.9 0.0 copy-done.9
  12.9 0.0 copy-start.2
  12.9 0.0 copy-start.3
  13.0 3.6 %local.1 = (f32[2048,128]{1,0:T(8,128)S(1)}, bf16[2048,128]{1,0:T(8,128)(2,1)S(1)}, f32[128,128]{1,0:T(8,128)S(1)}, f32[16,16,128]{2,1,0:T(8,128)S(1)}) custom-call(bf16[2048,128]{1,0:T(8,128)(2,1)S(1)} %bitcast.15, bf16[2048,128]{1,0:T(8,128)(2,1)S(1)} %bitcast.19, f32[16,128]{1,0:T(8,128)S(1)} %bitcast.32, f32[16,128]{1,0:T(8,128)S(1)} %bitcast.36), custom_call_target="tpu_custom_call" | custom-call | bytes 1 | tf_op jit(solution)/shard_map/local/pallas_call | solution.py:535
  16.5 0.0 collective-permute-done
  16.5 1.6 %collective-permute-done.1 = bf16[16,16,128]{2,1,0:T(8,128)(2,1)S(1)} collective-permute-done((bf16[16,16,128]{2,1,0:T(8,128)(2,1)S(1)}, bf16[16,16,128]{2,1,0:T(8,128)(2,1)S(1)}, u32[]{:S(2)}, u32[]{:S(2)}) %collective-permute-start.1) | collective-permute-done | bytes 65568 | tf_op jit(solution)/shard_map/ppermute | solution.py:452
  18.2 2.6 %collective-permute-done.2 = bf16[16,16,128]{2,1,0:T(8,128)(2,1)S(1)} collective-permute-done((bf16[16,16,128]{2,1,0:T(8,128)(2,1)S(1)}, bf16[16,16,128]{2,1,0:T(8,128)(2,1)S(1)}, u32[]{:S(2)}, u32[]{:S(2)}) %collective-permute-start.2) | collective-permute-done | bytes 65568 | tf_op jit(solution)/shard_map/ppermute | solution.py:452
  20.8 0.1 exponential_multiply_fusion.states.after_shard
  20.8 0.0 copy-done.2
  20.8 0.0 copy-done.3
  20.8 0.0 copy-start.8
  20.9 0.7 %middle.1 = (bf16[2048,128]{1,0:T(8,128)(2,1)S(1)}, f32[2048,128]{1,0:T(8,128)S(1)}) custom-call(f32[16,16,128]{2,1,0:T(8,128)S(1)} %exponential_multiply_fusion.states.after_shard, f32[2048,128]{1,0:T(8,128)S(1)} %get-tuple-element.35.local, bf16[2048,128]{1,0:T(8,128)(2,1)S(1)} %get-tuple-element.36.to_next, bf16[2048,128]{1,0:T(8,128)(2,1)S(1)} %bitcast.21, ...), custom_call_target="tpu_custom_call" | custom-call | bytes 1 | tf_op jit(solution)/shard_map/middle/pallas_call | solution.py:545
  21.5 0.0 copy-start.4
  21.5 1.4 %collective-permute-start.3 = (bf16[2048,128]{1,0:T(8,128)(2,1)S(1)}, bf16[2048,128]{1,0:T(8,128)(2,1)S(1)}, u32[]{:S(2)}, u32[]{:S(2)}) collective-permute-start(bf16[2048,128]{1,0:T(8,128)(2,1)S(1)} %get-tuple-element.37.dz1), channel_id=1, source_target_pairs={{8,0},{16,8},{24,16},{9,1},{17,9},{25,17},{10,2},{18,10},{26,18},{... | collective-permute-start | bytes 1572872 | tf_op jit(solution)/shard_map/ppermute | solution.py:452
  23.0 0.7 %table.1 = (bf16[2048,128]{1,0:T(8,128)(2,1)S(1)}, bf16[2048,128]{1,0:T(8,128)(2,1)S(1)}) custom-call(f32[16,128]{1,0:T(8,128)S(1)} %bitcast.33, bf16[2048,128]{1,0:T(8,128)(2,1)S(1)} %get-tuple-element.37.dz1), custom_call_target="tpu_custom_call" | custom-call | bytes 1 | tf_op jit(solution)/shard_map/table/pallas_call | solution.py:550
  23.7 0.0 collective-permute-done.4.before
  23.7 0.0 copy-done.8
  23.7 0.0 copy-done.4
  23.7 6.3 %forward.1 = (f32[2048,128]{1,0:T(8,128)S(1)}, bf16[2048,128]{1,0:T(8,128)(2,1)S(1)}, bf16[25,16,128]{2,1,0:T(8,128)(2,1)S(1)}) custom-call(bf16[2048,128]{1,0:T(8,128)(2,1)S(1)} %collective-permute-done.4.before, bf16[2048,128]{1,0:T(8,128)(2,1)S(1)} %copy-done.4, bf16[128,128]{1,0:T(8,128)(2,1)S(1)} %copy-done.8, bf16[2048,128]{1,0:T(8,128)(2,1)S(1)} %bitcast.25, ...), custom_call_target="tpu_custom_call" | custom-call | bytes 1 | tf_op jit(solution)/shard_map/forward/pallas_call | solution.py:556
  30.1 0.1 collective-permute-start.5
  30.2 3.1 %within.1 = (f32[2048,128]{1,0:T(8,128)S(1)}, bf16[2048,128]{1,0:T(8,128)(2,1)}, bf16[2048,128]{1,0:T(8,128)(2,1)}, f32[9,16,128]{2,1,0:T(8,128)S(1)}) custom-call(bf16[2048,128]{1,0:T(8,128)(2,1)S(1)} %get-tuple-element.43.u2, f32[128,128]{1,0:T(8,128)S(1)} %get-tuple-element.44.taps, f32[2048,128]{1,0:T(8,128)S(1)} %get-tuple-element.45.z1, ...), custom_call_target="tpu_custom_call" | custom-call | bytes 1 | tf_op jit(solution)/shard_map/within/pallas_call | solution.py:570
  33.3 0.0 collective-permute-done.5
  33.3 2.7 %collective-permute-start.6 = (bf16[25,16,128]{2,1,0:T(8,128)(2,1)S(1)}, bf16[25,16,128]{2,1,0:T(8,128)(2,1)S(1)}, u32[]{:S(2)}, u32[]{:S(2)}) collective-permute-start(bf16[25,16,128]{2,1,0:T(8,128)(2,1)S(1)} %pad_maximum_fusion), channel_id=1, source_target_pairs={{0,8},{8,0},{16,24},{24,16},{1,9},{9,1},{17,25},{25,17},{2,10},{10... | collective-permute-start | bytes 307208 | tf_op jit(solution)/shard_map/ppermute | solution.py:457
  36.0 0.0 collective-permute-done.3.later
  36.0 0.0 copy-start.6
  36.0 0.7 %factor.1 = (f32[9,16,128]{2,1,0:T(8,128)S(1)}, bf16[2048,128]{1,0:T(8,128)(2,1)S(1)}, f32[128,128]{1,0:T(8,128)S(1)}, f32[16,16,128]{2,1,0:T(8,128)S(1)}, f32[1...) custom-call(f32[16,16,128]{2,1,0:T(8,128)S(1)} %get-tuple-element.34.wide_rate, ...), custom_call_target="tpu_custom_call" | custom-call | bytes 1 | tf_op jit(solution)/shard_map/factor/pallas_call | solution.py:577
  36.7 0.0 copy-start.5
  36.7 2.8 %collective-permute-done.6 = bf16[25,16,128]{2,1,0:T(8,128)(2,1)S(1)} collective-permute-done((bf16[25,16,128]{2,1,0:T(8,128)(2,1)S(1)}, bf16[25,16,128]{2,1,0:T(8,128)(2,1)S(1)}, u32[]{:S(2)}, u32[]{:S(2)}) %collective-permute-start.6) | collective-permute-done | bytes 102432 | tf_op jit(solution)/shard_map/ppermute | solution.py:457
  39.6 0.8 %collective-permute-start.7 = (bf16[25,16,128]{2,1,0:T(8,128)(2,1)S(1)}, bf16[25,16,128]{2,1,0:T(8,128)(2,1)S(1)}, u32[]{:S(2)}, u32[]{:S(2)}) collective-permute-start(bf16[25,16,128]{2,1,0:T(8,128)(2,1)S(1)} %pad_maximum_fusion.1), channel_id=1, source_target_pairs={{0,16},{8,24},{16,0},{24,8},{1,17},{9,25},{17,1},{25,9},{2,18},{10... | collective-permute-start | bytes 307208 | tf_op jit(solution)/shard_map/ppermute | solution.py:457
  40.4 0.0 copy-done.6
  40.5 0.0 copy-done.5
  40.5 3.3 %product.1 = (bf16[2048,128]{1,0:T(8,128)(2,1)}, bf16[2048,128]{1,0:T(8,128)(2,1)}) custom-call(bf16[2048,128]{1,0:T(8,128)(2,1)S(1)} %get-tuple-element.37.dz1, bf16[2048,128]{1,0:T(8,128)(2,1)S(1)} %collective-permute-done.3.later, f32[128,128]{1,0:T(8,128)S(1)} %get-tuple-element.38.turned, bf16[2048,128]{1,0:T(8,128)(2,1)S(1)} %bitcast.28, ...), custom_call_target="tpu_custom_call" | custom-call | bytes 1 | tf_op jit(solution)/shard_map/product/pallas_call | solution.py:583
  43.7 3.8 %collective-permute-done.7 = bf16[25,16,128]{2,1,0:T(8,128)(2,1)S(1)} collective-permute-done((bf16[25,16,128]{2,1,0:T(8,128)(2,1)S(1)}, bf16[25,16,128]{2,1,0:T(8,128)(2,1)S(1)}, u32[]{:S(2)}, u32[]{:S(2)}) %collective-permute-start.7) | collective-permute-done | bytes 102432 | tf_op jit(solution)/shard_map/ppermute | solution.py:457
  47.5 1.8 %value.1 = (bf16[2048,128]{1,0:T(8,128)(2,1)}, f32[128,128]{1,0:T(8,128)}, f32[16,128]{1,0:T(8,128)}) custom-call(f32[16,16,128]{2,1,0:T(8,128)S(1)} %fusion.states, bf16[2048,128]{1,0:T(8,128)(2,1)S(1)} %get-tuple-element.56.after, f32[2048,128]{1,0:T(8,128)S(1)} %get-tuple-element.57.z2, bf16[2048,128]{1,0:T(8,128)(2,1)S(1)} %bitcast.17, ...), custom_call_target="tpu_custom_call" | custom-call | bytes 1 | tf_op jit(solution)/shard_map/value/pallas_call | solution.py:607
  (9 shorter events, 0.2 us)
Async XLA Ops:
  0.6 7.2 %copy-start = (bf16[1,2048,128]{2,1,0:T(8,128)(2,1)S(1)}, bf16[1,2048,128]{2,1,0:T(8,128)(2,1)}, u32[]{:S(2)}) copy-start(bf16[1,2048,128]{2,1,0:T(8,128)(2,1)} %param.14) | copy-start | bytes 1572868
  0.6 7.2 %copy-start.1 = (bf16[1,2048,128]{2,1,0:T(8,128)(2,1)S(1)}, bf16[1,2048,128]{2,1,0:T(8,128)(2,1)}, u32[]{:S(2)}) copy-start(bf16[1,2048,128]{2,1,0:T(8,128)(2,1)} %param.13) | copy-start | bytes 1572868
  0.7 7.2 %copy-start.7 = (f32[128,16]{0,1:T(8,128)S(1)}, f32[128,16]{0,1:T(8,128)}, u32[]{:S(2)}) copy-start(f32[128,16]{0,1:T(8,128)} %param.17) | copy-start | bytes 24580
  2.8 20.8 %collective-permute-start.4 = (bf16[2048,128]{1,0:T(8,128)(2,1)}, bf16[2048,128]{1,0:T(8,128)(2,1)S(1)}, u32[]{:S(2)}, u32[]{:S(2)}) collective-permute-start(bf16[2048,128]{1,0:T(8,128)(2,1)} %gate.1.now), channel_id=1, source_target_pairs={{0,8},{8,16},{16,24},{1,9},{9,17},{17,25},{2,10},{10,18},{18,26},{... | collective-permute-start | bytes 1572872 | tf_op jit(solution)/shard_map/ppermute | solution.py:452
  7.8 5.1 %copy-start.9 = (f32[128,16]{0,1:T(8,128)S(1)}, f32[128,16]{0,1:T(8,128)}, u32[]{:S(2)}) copy-start(f32[128,16]{0,1:T(8,128)} %param.16) | copy-start | bytes 24580
  9.0 7.5 %collective-permute-start = (bf16[16,16,128]{2,1,0:T(8,128)(2,1)S(1)}, bf16[16,16,128]{2,1,0:T(8,128)(2,1)S(1)}, u32[]{:S(2)}, u32[]{:S(2)}) collective-permute-start(bf16[16,16,128]{2,1,0:T(8,128)(2,1)S(1)} %state.1), channel_id=1, source_target_pairs={{8,0},{16,8},{24,16},{9,1},{17,9},{25,17},{10,2},{18,10},{26,18},{... | collective-permute-start | bytes 196616 | tf_op jit(solution)/shard_map/ppermute | solution.py:452
  10.3 7.8 %collective-permute-start.1 = (bf16[16,16,128]{2,1,0:T(8,128)(2,1)S(1)}, bf16[16,16,128]{2,1,0:T(8,128)(2,1)S(1)}, u32[]{:S(2)}, u32[]{:S(2)}) collective-permute-start(bf16[16,16,128]{2,1,0:T(8,128)(2,1)S(1)} %state.1), channel_id=1, source_target_pairs={{16,0},{24,8},{17,1},{25,9},{18,2},{26,10},{19,3},{27,11},{20,4},{... | collective-permute-start | bytes 196616 | tf_op jit(solution)/shard_map/ppermute | solution.py:452
  11.6 9.1 %collective-permute-start.2 = (bf16[16,16,128]{2,1,0:T(8,128)(2,1)S(1)}, bf16[16,16,128]{2,1,0:T(8,128)(2,1)S(1)}, u32[]{:S(2)}, u32[]{:S(2)}) collective-permute-start(bf16[16,16,128]{2,1,0:T(8,128)(2,1)S(1)} %state.1), channel_id=1, source_target_pairs={{24,0},{25,1},{26,2},{27,3},{28,4},{29,5},{30,6},{31,7}} | collective-permute-start | bytes 196616 | tf_op jit(solution)/shard_map/ppermute | solution.py:452
  12.9 7.9 %copy-start.2 = (bf16[1,2048,128]{2,1,0:T(8,128)(2,1)S(1)}, bf16[1,2048,128]{2,1,0:T(8,128)(2,1)}, u32[]{:S(2)}) copy-start(bf16[1,2048,128]{2,1,0:T(8,128)(2,1)} %param.12) | copy-start | bytes 1572868
  12.9 7.9 %copy-start.3 = (bf16[1,2048,128]{2,1,0:T(8,128)(2,1)S(1)}, bf16[1,2048,128]{2,1,0:T(8,128)(2,1)}, u32[]{:S(2)}) copy-start(bf16[1,2048,128]{2,1,0:T(8,128)(2,1)} %param.11) | copy-start | bytes 1572868
  20.8 2.8 %copy-start.8 = (bf16[128,128]{1,0:T(8,128)(2,1)S(1)}, bf16[128,128]{1,0:T(8,128)(2,1)}, u32[]{:S(2)}) copy-start(bf16[128,128]{1,0:T(8,128)(2,1)} %filters.3) | copy-start | bytes 98308
  21.5 2.2 %copy-start.4 = (bf16[2048,128]{1,0:T(8,128)(2,1)S(1)}, bf16[2048,128]{1,0:T(8,128)(2,1)}, u32[]{:S(2)}) copy-start(bf16[2048,128]{1,0:T(8,128)(2,1)} %gate.1.now) | copy-start | bytes 1572868
  21.5 14.5 %collective-permute-start.3 = (bf16[2048,128]{1,0:T(8,128)(2,1)S(1)}, bf16[2048,128]{1,0:T(8,128)(2,1)S(1)}, u32[]{:S(2)}, u32[]{:S(2)}) collective-permute-start(bf16[2048,128]{1,0:T(8,128)(2,1)S(1)} %get-tuple-element.37.dz1), channel_id=1, source_target_pairs={{8,0},{16,8},{24,16},{9,1},{17,9},{25,17},{10,2},{18,10},{26,18},{... | collective-permute-start | bytes 1572872 | tf_op jit(solution)/shard_map/ppermute | solution.py:452
  30.1 3.2 %collective-permute-start.5 = (bf16[9,16,128]{2,1,0:T(8,128)(2,1)S(1)}, bf16[9,16,128]{2,1,0:T(8,128)(2,1)S(1)}, u32[]{:S(2)}, u32[]{:S(2)}) collective-permute-start(bf16[9,16,128]{2,1,0:T(8,128)(2,1)S(1)} %slice.19), channel_id=1, source_target_pairs={{0,1},{1,0},{2,3},{3,2},{4,5},{5,4},{6,7},{7,6},{8,9},{9,8},{10,11... | collective-permute-start | bytes 110600 | tf_op jit(solution)/shard_map/ppermute | solution.py:457
  33.3 6.2 %collective-permute-start.6 = (bf16[25,16,128]{2,1,0:T(8,128)(2,1)S(1)}, bf16[25,16,128]{2,1,0:T(8,128)(2,1)S(1)}, u32[]{:S(2)}, u32[]{:S(2)}) collective-permute-start(bf16[25,16,128]{2,1,0:T(8,128)(2,1)S(1)} %pad_maximum_fusion), channel_id=1, source_target_pairs={{0,8},{8,0},{16,24},{24,16},{1,9},{9,1},{17,25},{25,17},{2,10},{10... | collective-permute-start | bytes 307208 | tf_op jit(solution)/shard_map/ppermute | solution.py:457
  36.0 4.4 %copy-start.6 = (bf16[1,2048,128]{2,1,0:T(8,128)(2,1)S(1)}, bf16[1,2048,128]{2,1,0:T(8,128)(2,1)}, u32[]{:S(2)}) copy-start(bf16[1,2048,128]{2,1,0:T(8,128)(2,1)} %param.10) | copy-start | bytes 1572868
  36.7 3.7 %copy-start.5 = (bf16[1,2048,128]{2,1,0:T(8,128)(2,1)S(1)}, bf16[1,2048,128]{2,1,0:T(8,128)(2,1)}, u32[]{:S(2)}) copy-start(bf16[1,2048,128]{2,1,0:T(8,128)(2,1)} %param.9) | copy-start | bytes 1572868
  39.6 7.9 %collective-permute-start.7 = (bf16[25,16,128]{2,1,0:T(8,128)(2,1)S(1)}, bf16[25,16,128]{2,1,0:T(8,128)(2,1)S(1)}, u32[]{:S(2)}, u32[]{:S(2)}) collective-permute-start(bf16[25,16,128]{2,1,0:T(8,128)(2,1)S(1)} %pad_maximum_fusion.1), channel_id=1, source_target_pairs={{0,16},{8,24},{16,0},{24,8},{1,17},{9,25},{17,1},{25,9},{2,18},{10... | collective-permute-start | bytes 307208 | tf_op jit(solution)/shard_map/ppermute | solution.py:457
where the time goes:
time: 49.6 us; the launch traced here: 49.3 us
  Pallas kernels  23.4 us (47%)
  starting transfers between devices  13.9 us (28%)
  waiting for transfers between devices  10.8 us (22%)
  between operations  0.94 us (2%)
    ppermute x5, starting transfers between devices, shifted(): lax.ppermute(value, axis, [(source, source + steps) for source in range(f...  10.3 us
    ppermute x3, waiting for transfers between devices, swapped(): lax.ppermute(value, axis, [(source, source ^ bit) for source in range(cou...  6.59 us
    pallas_call x1, Pallas kernels, per_device(): call(forward_kernel, 'forward', [twice(spec) for spec in [wide, wide, tab...  6.35 us
    ppermute x5, waiting for transfers between devices, shifted(): lax.ppermute(value, axis, [(source, source + steps) for source in range(f...  4.23 us
    ppermute x3, starting transfers between devices, swapped(): lax.ppermute(value, axis, [(source, source ^ bit) for source in range(cou...  3.6 us
    pallas_call x1, Pallas kernels, per_device(): call(local_kernel, 'local', [wide, wide, modes, modes], [wide, wide, tabl...  3.56 us
    pallas_call x1, Pallas kernels, per_device(): call(product_kernel, 'product', [twice(spec) for spec in (wide, wide, tab...  3.25 us
    pallas_call x1, Pallas kernels, per_device(): call(within_kernel, 'within', [wide, table, wide, wide, wide, wide], [wid...  3.1 us
  transfers between devices with their start and end apart: 8, of which 4 were waited for; matrix products, arithmetic and copies ran while one was open for 0% of the time, Pallas kernels for 39%

commit v1 on v0

--- a/solution.py
+++ b/solution.py
@@ -208,51 +208,44 @@
     return table[pl.ds(block * PACK, PACK), :]
 
 
-def local_kernel(grad, value, rate, residue, du2, to_next, taps, wide_rate):
+def table_kernel(rate, residue, to_next, to_end, power, taps, turned, wide_rate):
     rows, cols = iotas()
     mask = rows // LANES == cols // LANES
     offsets = cols.astype(F32)
+    lags = ((CHUNK - 1 - cols) % TILE).astype(F32)
     at = pl.program_id(0)
-    blocks = wide_rate.shape[0]
+    blocks = power.shape[0] // TILE
     coeffs = residue[...] * jnp.sqrt(one_minus_exp(2.0 * rate[...]))
-    owns = [block_groups(at, blocks, block) for block in range(blocks)]
-    rates = [column(rate[...], own) for own in owns]
-    scales = [column(coeffs, own) for own in owns]
-    sums = [
-        jnp.sum((jnp.exp(-each * offsets) * scale).reshape(PACK, LANES, TILE), axis=1)
-        for each, scale in zip(rates, scales)
-    ]
+    sums = []
+    for block in range(blocks):
+        span = pl.ds(block * TILE, TILE)
+        own = block_groups(at, blocks, block)
+        rates = column(rate[...], own)
+        scale = column(coeffs, own)
+        wide_rate[block] = squeeze_groups(jnp.broadcast_to(rates, (TILE, TILE)), mask)
+        scaled = jnp.exp(-rates * offsets) * scale
+        ends = jnp.exp(-rates * (TILE - 1 - offsets))
+        power[span, :] = jnp.exp(-rates * lags).astype(BF16)
+        to_end[span, :] = ends.astype(BF16)
+        to_next[span, :] = (ends * scale).astype(BF16)
+        sums.append(jnp.sum(scaled.reshape(PACK, LANES, TILE), axis=1))
     taps[...] = above(*sums)
-    turned = nn(above(*sums).astype(BF16), reversal())
+    turned[...] = nn(above(*sums).astype(BF16), reversal())
+
+
+def local_kernel(grad, value, turned, du2):
+    rows, cols = iotas()
     lower = ones_where(rows >= cols)
     lower_half = beside(lower, lower)
-    for block, span in enumerate(spans(grad)):
-        wide_rate[block] = squeeze_groups(jnp.broadcast_to(rates[block], (TILE, TILE)), mask)
-        ends = jnp.exp(-rates[block] * (TILE - 1 - offsets))
-        to_next[span, :] = (ends * scales[block]).astype(BF16)
     results = [
-        within_shard(
-            grad[span, :] * value[span, :], turned[block * PACK : (block + 1) * PACK], lower_half
-        )
+        within_shard(grad[span, :] * value[span, :], group_rows(turned, block), lower_half)
         for block, span in enumerate(spans(grad))
     ]
     for span, result in zip(spans(grad), results):
         du2[span, :] = result
 
 
-def table_kernel(rate, dz1, to_end, power):
-    _, cols = iotas()
-    offsets = cols.astype(F32)
-    lags = ((CHUNK - 1 - cols) % TILE).astype(F32)
-    at = pl.program_id(0)
-    blocks = power.shape[0] // TILE
-    for block, span in enumerate(spans(power)):
-        rates = column(rate[...], block_groups(at, blocks, block))
-        power[span, :] = jnp.exp(-rates * lags).astype(BF16)
-        to_end[span, :] = jnp.exp(-rates * (TILE - 1 - offsets)).astype(BF16)
-
-
-def middle_kernel(states, local, to_next, li_key, value, dz1, du2):
+def middle_kernel(states, local, to_next, li_key, value, before, dz1, du2):
     rows, cols = iotas()
     mask = rows // LANES == cols // LANES
     wides = [spread_groups(states[block], mask).T.astype(BF16) for block in range(states.shape[0])]
@@ -532,10 +525,13 @@
     )
 
     later_backs = [shifted(back, "seq", -gap) for gap in range(1, lax.axis_size("seq"))]
-    du2_local, to_next, taps, wide_rate = call(
-        local_kernel, "local", [wide, wide, modes, modes], [wide, wide, table, chunk],
-        [wide_full, wide_half, table_full, chunk_full],
-    )(grad, value_two, rate, residue)
+    to_next, to_end, power, taps, turned, wide_rate = call(
+        table_kernel, "table", [modes, modes], [wide] * 3 + [table] * 2 + [chunk],
+        [wide_half] * 3 + [table_full] * 2 + [chunk_full],
+    )(rate, residue)
+    (du2_local,) = call(local_kernel, "local", [wide, wide, table], [wide], [wide_full])(
+        grad, value_two, turned
+    )
     fade = jnp.exp(-TILE * wide_rate)
     after_shard = later_backs[-1].astype(F32)
     for other in later_backs[-2::-1]:
@@ -543,13 +539,11 @@
     after_shard = after_shard * jnp.exp(-wide_rate)
 
     dz1, du2 = call(
-        middle_kernel, "middle", [twice(chunk)] + [twice(wide)] * 4, [twice(wide)] * 2,
+        middle_kernel, "middle", [twice(chunk)] + [twice(wide)] * 4 + [anywhere],
+        [twice(wide)] * 2,
         [wide_half, wide_full], grid=STEPS // 2,
-    )(after_shard, du2_local, to_next, key_two, value)
+    )(after_shard, du2_local, to_next, key_two, value, product_before)
     dz1_later = shifted(dz1, "seq", -1)
-    to_end, power = call(
-        table_kernel, "table", [modes, anywhere], [wide, wide], [wide_half, wide_half]
-    )(rate, dz1)
 
     filter_chunks = groups // LANES
     packed_shape = jax.ShapeDtypeStruct((blocks + filter_chunks + 1, LANES, TILE), BF16)

time: 49.6 us -> 47.8 us (0.964)
  waiting for transfers between devices: 10.8 us -> 7.5 us
  starting transfers between devices: 13.9 us -> 15.9 us
    ppermute x3, waiting for transfers between devices: 6.59 us -> 3.41 us  [swapped(): lax.ppermute(value, axis, [(source, source ^ bit) for source in range(cou...]
    ppermute x3, starting transfers between devices: 3.6 us -> 5.78 us  [swapped(): lax.ppermute(value, axis, [(source, source ^ bit) for source in range(cou...]
  transfers between devices with their start and end apart: 8 -> 8, of which waited for: 4 -> 5; matrix products, arithmetic and copies ran while one was open for 0% -> 0% of each run, Pallas kernels for 39% -> 39%
where the time goes in v1:
time: 47.8 us; the launch traced here: 47.6 us
  Pallas kernels  23 us (48%)
  starting transfers between devices  15.9 us (33%)
  waiting for transfers between devices  7.5 us (16%)
  between operations  0.92 us (2%)
    ppermute x5, starting transfers between devices, shifted(): lax.ppermute(value, axis, [(source, source + steps) for source in range(f...  10.1 us
    pallas_call x1, Pallas kernels, per_device(): call(forward_kernel, 'forward', [twice(spec) for spec in [wide, wide, tab...  6.34 us
    ppermute x3, starting transfers between devices, swapped(): lax.ppermute(value, axis, [(source, source ^ bit) for source in range(cou...  5.78 us
    ppermute x5, waiting for transfers between devices, shifted(): lax.ppermute(value, axis, [(source, source + steps) for source in range(f...  4.09 us
    ppermute x3, waiting for transfers between devices, swapped(): lax.ppermute(value, axis, [(source, source ^ bit) for source in range(cou...  3.41 us
    pallas_call x1, Pallas kernels, per_device(): call(product_kernel, 'product', [twice(spec) for spec in (wide, wide, tab...  3.27 us
    pallas_call x1, Pallas kernels, per_device(): call(within_kernel, 'within', [wide, table, wide, wide, wide, wide], [wid...  3.1 us
    pallas_call x1, Pallas kernels, per_device(): call(local_kernel, 'local', [wide, wide, table], [wide], [wide_full])  2.26 us
  transfers between devices with their start and end apart: 8, of which 5 were waited for; matrix products, arithmetic and copies ran while one was open for 0% of the time, Pallas kernels for 39%

profile of v1, /device:TPU:0, one launch (start us, length us, event | category | flops | bytes accessed | tf_op | source)
XLA Modules:
  0.0 47.6 jit_solution(8056318907250718829)
XLA Ops:
  0.6 0.0 copy-start
  0.6 0.0 copy-start.3
  0.7 0.0 copy-start.7
  0.7 2.2 %gate.1.now = bf16[2048,128]{1,0:T(8,128)(2,1)} custom-call(bf16[2048,128]{1,0:T(8,128)(2,1)} %bitcast.27, bf16[2048,128]{1,0:T(8,128)(2,1)} %bitcast.29), custom_call_target="tpu_custom_call" | custom-call | bytes 1 | tf_op jit(solution)/shard_map/gate/pallas_call | solution.py:513
  2.8 5.0 %collective-permute-start.3 = (bf16[2048,128]{1,0:T(8,128)(2,1)}, bf16[2048,128]{1,0:T(8,128)(2,1)S(1)}, u32[]{:S(2)}, u32[]{:S(2)}) collective-permute-start(bf16[2048,128]{1,0:T(8,128)(2,1)} %gate.1.now), channel_id=1, source_target_pairs={{0,8},{8,16},{16,24},{1,9},{9,17},{17,25},{2,10},{10,18},{18,26},{... | collective-permute-start | bytes 1572872 | tf_op jit(solution)/shard_map/ppermute | solution.py:445
  7.8 0.0 copy-done
  7.8 0.0 copy-done.3
  7.8 0.0 copy-done.7
  7.8 0.0 copy-start.9
  7.8 1.2 %state.1 = bf16[16,16,128]{2,1,0:T(8,128)(2,1)S(1)} custom-call(bf16[2048,128]{1,0:T(8,128)(2,1)S(1)} %bitcast.14, bf16[2048,128]{1,0:T(8,128)(2,1)S(1)} %bitcast.24, f32[16,128]{1,0:T(8,128)S(1)} %bitcast.31), custom_call_target="tpu_custom_call" | custom-call | bytes 1 | tf_op jit(solution)/shard_map/state/pallas_call | solution.py:523
  9.0 1.3 %collective-permute-start.2 = (bf16[16,16,128]{2,1,0:T(8,128)(2,1)S(1)}, bf16[16,16,128]{2,1,0:T(8,128)(2,1)S(1)}, u32[]{:S(2)}, u32[]{:S(2)}) collective-permute-start(bf16[16,16,128]{2,1,0:T(8,128)(2,1)S(1)} %state.1), channel_id=1, source_target_pairs={{24,0},{25,1},{26,2},{27,3},{28,4},{29,5},{30,6},{31,7}} | collective-permute-start | bytes 196616 | tf_op jit(solution)/shard_map/ppermute | solution.py:445
  10.3 1.3 %collective-permute-start.1 = (bf16[16,16,128]{2,1,0:T(8,128)(2,1)S(1)}, bf16[16,16,128]{2,1,0:T(8,128)(2,1)S(1)}, u32[]{:S(2)}, u32[]{:S(2)}) collective-permute-start(bf16[16,16,128]{2,1,0:T(8,128)(2,1)S(1)} %state.1), channel_id=1, source_target_pairs={{16,0},{24,8},{17,1},{25,9},{18,2},{26,10},{19,3},{27,11},{20,4},{... | collective-permute-start | bytes 196616 | tf_op jit(solution)/shard_map/ppermute | solution.py:445
  11.6 1.3 %collective-permute-start = (bf16[16,16,128]{2,1,0:T(8,128)(2,1)S(1)}, bf16[16,16,128]{2,1,0:T(8,128)(2,1)S(1)}, u32[]{:S(2)}, u32[]{:S(2)}) collective-permute-start(bf16[16,16,128]{2,1,0:T(8,128)(2,1)S(1)} %state.1), channel_id=1, source_target_pairs={{8,0},{16,8},{24,16},{9,1},{17,9},{25,17},{10,2},{18,10},{26,18},{... | collective-permute-start | bytes 196616 | tf_op jit(solution)/shard_map/ppermute | solution.py:445
  12.9 0.0 copy-done.9
  12.9 1.6 %table.1 = (bf16[2048,128]{1,0:T(8,128)(2,1)S(1)}, bf16[2048,128]{1,0:T(8,128)(2,1)S(1)}, bf16[2048,128]{1,0:T(8,128)(2,1)S(1)}, f32[128,128]{1,0:T(8,128)S(1)},...) custom-call(f32[16,128]{1,0:T(8,128)S(1)} %bitcast.32, f32[16,128]{1,0:T(8,128)S(1)} %bitcast.35), custom_call_target="tpu_custom_call" | custom-call | bytes 1 | tf_op jit(solution)/shard_map/table/pallas_call | solution.py:528
  14.5 0.0 copy-start.1
  14.5 0.0 copy-start.2
  14.5 2.3 %local.1 = f32[2048,128]{1,0:T(8,128)S(1)} custom-call(bf16[2048,128]{1,0:T(8,128)(2,1)S(1)} %bitcast.15, bf16[2048,128]{1,0:T(8,128)(2,1)S(1)} %bitcast.25, f32[128,128]{1,0:T(8,128)S(1)} %get-tuple-element.35.turned), custom_call_target="tpu_custom_call" | custom-call | bytes 1 | tf_op jit(solution)/shard_map/local/pallas_call | solution.py:532
  16.8 0.9 %collective-permute-done.2 = bf16[16,16,128]{2,1,0:T(8,128)(2,1)S(1)} collective-permute-done((bf16[16,16,128]{2,1,0:T(8,128)(2,1)S(1)}, bf16[16,16,128]{2,1,0:T(8,128)(2,1)S(1)}, u32[]{:S(2)}, u32[]{:S(2)}) %collective-permute-start.2) | collective-permute-done | bytes 65568 | tf_op jit(solution)/shard_map/ppermute | solution.py:445
  17.7 2.1 %collective-permute-done.1 = bf16[16,16,128]{2,1,0:T(8,128)(2,1)S(1)} collective-permute-done((bf16[16,16,128]{2,1,0:T(8,128)(2,1)S(1)}, bf16[16,16,128]{2,1,0:T(8,128)(2,1)S(1)}, u32[]{:S(2)}, u32[]{:S(2)}) %collective-permute-start.1) | collective-permute-done | bytes 65568 | tf_op jit(solution)/shard_map/ppermute | solution.py:445
  19.8 0.0 collective-permute-done
  19.8 0.1 exponential_multiply_fusion.states.after_shard
  19.8 0.0 collective-permute-done.3.before
  19.8 0.0 copy-done.1
  19.9 0.0 copy-done.2
  19.9 0.0 copy-start.4
  19.9 0.0 copy-start.8
  19.9 0.7 %middle.1 = (bf16[2048,128]{1,0:T(8,128)(2,1)S(1)}, f32[2048,128]{1,0:T(8,128)S(1)}) custom-call(f32[16,16,128]{2,1,0:T(8,128)S(1)} %exponential_multiply_fusion.states.after_shard, f32[2048,128]{1,0:T(8,128)S(1)} %local.1, bf16[2048,128]{1,0:T(8,128)(2,1)S(1)} %get-tuple-element.36.to_next, bf16[2048,128]{1,0:T(8,128)(2,1)S(1)} %bitcast.18, ...), custom_call_target="tpu_custom_call" | custom-call | bytes 1 | tf_op jit(solution)/shard_map/middle/pallas_call | solution.py:541
  20.6 1.3 %collective-permute-start.4 = (bf16[2048,128]{1,0:T(8,128)(2,1)S(1)}, bf16[2048,128]{1,0:T(8,128)(2,1)S(1)}, u32[]{:S(2)}, u32[]{:S(2)}) collective-permute-start(bf16[2048,128]{1,0:T(8,128)(2,1)S(1)} %get-tuple-element.37.dz1), channel_id=1, source_target_pairs={{8,0},{16,8},{24,16},{9,1},{17,9},{25,17},{10,2},{18,10},{26,18},{... | collective-permute-start | bytes 1572872 | tf_op jit(solution)/shard_map/ppermute | solution.py:445
  21.9 0.0 copy-done.4
  21.9 0.0 copy-done.8
  21.9 6.3 %forward.1 = (f32[2048,128]{1,0:T(8,128)S(1)}, bf16[2048,128]{1,0:T(8,128)(2,1)S(1)}, bf16[25,16,128]{2,1,0:T(8,128)(2,1)S(1)}) custom-call(bf16[2048,128]{1,0:T(8,128)(2,1)S(1)} %collective-permute-done.3.before, bf16[2048,128]{1,0:T(8,128)(2,1)S(1)} %copy-done.4, bf16[128,128]{1,0:T(8,128)(2,1)S(1)} %copy-done.8, bf16[2048,128]{1,0:T(8,128)(2,1)S(1)} %bitcast.22, ...), custom_call_target="tpu_custom_call" | custom-call | bytes 1 | tf_op jit(solution)/shard_map/forward/pallas_call | solution.py:550
  28.2 0.1 collective-permute-start.5
  28.3 3.1 %within.1 = (f32[2048,128]{1,0:T(8,128)S(1)}, bf16[2048,128]{1,0:T(8,128)(2,1)}, bf16[2048,128]{1,0:T(8,128)(2,1)}, f32[9,16,128]{2,1,0:T(8,128)S(1)}) custom-call(bf16[2048,128]{1,0:T(8,128)(2,1)S(1)} %get-tuple-element.43.u2, f32[128,128]{1,0:T(8,128)S(1)} %get-tuple-element.44.taps, f32[2048,128]{1,0:T(8,128)S(1)} %get-tuple-element.45.z1, ...), custom_call_target="tpu_custom_call" | custom-call | bytes 1 | tf_op jit(solution)/shard_map/within/pallas_call | solution.py:564
  31.4 0.0 collective-permute-done.5
  31.5 2.7 %collective-permute-start.6 = (bf16[25,16,128]{2,1,0:T(8,128)(2,1)S(1)}, bf16[25,16,128]{2,1,0:T(8,128)(2,1)S(1)}, u32[]{:S(2)}, u32[]{:S(2)}) collective-permute-start(bf16[25,16,128]{2,1,0:T(8,128)(2,1)S(1)} %pad_maximum_fusion), channel_id=1, source_target_pairs={{0,8},{8,0},{16,24},{24,16},{1,9},{9,1},{17,25},{25,17},{2,10},{10... | collective-permute-start | bytes 307208 | tf_op jit(solution)/shard_map/ppermute | solution.py:450
  34.2 1.1 %collective-permute-done.4.later = bf16[2048,128]{1,0:T(8,128)(2,1)S(1)} collective-permute-done((bf16[2048,128]{1,0:T(8,128)(2,1)S(1)}, bf16[2048,128]{1,0:T(8,128)(2,1)S(1)}, u32[]{:S(2)}, u32[]{:S(2)}) %collective-permute-start.4) | collective-permute-done | bytes 524320 | tf_op jit(solution)/shard_map/ppermute | solution.py:445
  35.3 0.0 copy-start.6
  35.3 0.7 %factor.1 = (f32[9,16,128]{2,1,0:T(8,128)S(1)}, bf16[2048,128]{1,0:T(8,128)(2,1)S(1)}, f32[128,128]{1,0:T(8,128)S(1)}, f32[16,16,128]{2,1,0:T(8,128)S(1)}, f32[1...) custom-call(f32[16,16,128]{2,1,0:T(8,128)S(1)} %get-tuple-element.34.wide_rate, ...), custom_call_target="tpu_custom_call" | custom-call | bytes 1 | tf_op jit(solution)/shard_map/factor/pallas_call | solution.py:571
  36.0 0.0 copy-start.5
  36.0 1.7 %collective-permute-done.6 = bf16[25,16,128]{2,1,0:T(8,128)(2,1)S(1)} collective-permute-done((bf16[25,16,128]{2,1,0:T(8,128)(2,1)S(1)}, bf16[25,16,128]{2,1,0:T(8,128)(2,1)S(1)}, u32[]{:S(2)}, u32[]{:S(2)}) %collective-permute-start.6) | collective-permute-done | bytes 102432 | tf_op jit(solution)/shard_map/ppermute | solution.py:450
  37.8 3.0 %collective-permute-start.7 = (bf16[25,16,128]{2,1,0:T(8,128)(2,1)S(1)}, bf16[25,16,128]{2,1,0:T(8,128)(2,1)S(1)}, u32[]{:S(2)}, u32[]{:S(2)}) collective-permute-start(bf16[25,16,128]{2,1,0:T(8,128)(2,1)S(1)} %pad_maximum_fusion.1), channel_id=1, source_target_pairs={{0,16},{8,24},{16,0},{24,8},{1,17},{9,25},{17,1},{25,9},{2,18},{10... | collective-permute-start | bytes 307208 | tf_op jit(solution)/shard_map/ppermute | solution.py:450
  40.8 0.0 copy-done.6
  40.8 0.0 copy-done.5
  40.8 3.3 %product.1 = (bf16[2048,128]{1,0:T(8,128)(2,1)}, bf16[2048,128]{1,0:T(8,128)(2,1)}) custom-call(bf16[2048,128]{1,0:T(8,128)(2,1)S(1)} %get-tuple-element.37.dz1, bf16[2048,128]{1,0:T(8,128)(2,1)S(1)} %collective-permute-done.4.later, f32[128,128]{1,0:T(8,128)S(1)} %get-tuple-element.38.turned, bf16[2048,128]{1,0:T(8,128)(2,1)S(1)} %bitcast.28, ...), custom_call_target="tpu_custom_call" | custom-call | bytes 1 | tf_op jit(solution)/shard_map/product/pallas_call | solution.py:577
  44.1 1.7 %collective-permute-done.7 = bf16[25,16,128]{2,1,0:T(8,128)(2,1)S(1)} collective-permute-done((bf16[25,16,128]{2,1,0:T(8,128)(2,1)S(1)}, bf16[25,16,128]{2,1,0:T(8,128)(2,1)S(1)}, u32[]{:S(2)}, u32[]{:S(2)}) %collective-permute-start.7) | collective-permute-done | bytes 102432 | tf_op jit(solution)/shard_map/ppermute | solution.py:450
  45.8 1.8 %value.1 = (bf16[2048,128]{1,0:T(8,128)(2,1)}, f32[128,128]{1,0:T(8,128)}, f32[16,128]{1,0:T(8,128)}) custom-call(f32[16,16,128]{2,1,0:T(8,128)S(1)} %fusion.states, bf16[2048,128]{1,0:T(8,128)(2,1)S(1)} %get-tuple-element.56.after, f32[2048,128]{1,0:T(8,128)S(1)} %get-tuple-element.57.z2, bf16[2048,128]{1,0:T(8,128)(2,1)S(1)} %bitcast.17, ...), custom_call_target="tpu_custom_call" | custom-call | bytes 1 | tf_op jit(solution)/shard_map/value/pallas_call | solution.py:601
  (9 shorter events, 0.2 us)
Async XLA Ops:
  0.6 7.2 %copy-start = (bf16[1,2048,128]{2,1,0:T(8,128)(2,1)S(1)}, bf16[1,2048,128]{2,1,0:T(8,128)(2,1)}, u32[]{:S(2)}) copy-start(bf16[1,2048,128]{2,1,0:T(8,128)(2,1)} %param.14) | copy-start | bytes 1572868
  0.6 7.2 %copy-start.3 = (bf16[1,2048,128]{2,1,0:T(8,128)(2,1)S(1)}, bf16[1,2048,128]{2,1,0:T(8,128)(2,1)}, u32[]{:S(2)}) copy-start(bf16[1,2048,128]{2,1,0:T(8,128)(2,1)} %param.13) | copy-start | bytes 1572868
  0.7 7.2 %copy-start.7 = (f32[128,16]{0,1:T(8,128)S(1)}, f32[128,16]{0,1:T(8,128)}, u32[]{:S(2)}) copy-start(f32[128,16]{0,1:T(8,128)} %param.17) | copy-start | bytes 24580
  2.8 17.0 %collective-permute-start.3 = (bf16[2048,128]{1,0:T(8,128)(2,1)}, bf16[2048,128]{1,0:T(8,128)(2,1)S(1)}, u32[]{:S(2)}, u32[]{:S(2)}) collective-permute-start(bf16[2048,128]{1,0:T(8,128)(2,1)} %gate.1.now), channel_id=1, source_target_pairs={{0,8},{8,16},{16,24},{1,9},{9,17},{17,25},{2,10},{10,18},{18,26},{... | collective-permute-start | bytes 1572872 | tf_op jit(solution)/shard_map/ppermute | solution.py:445
  7.8 5.1 %copy-start.9 = (f32[128,16]{0,1:T(8,128)S(1)}, f32[128,16]{0,1:T(8,128)}, u32[]{:S(2)}) copy-start(f32[128,16]{0,1:T(8,128)} %param.16) | copy-start | bytes 24580
  9.0 8.7 %collective-permute-start.2 = (bf16[16,16,128]{2,1,0:T(8,128)(2,1)S(1)}, bf16[16,16,128]{2,1,0:T(8,128)(2,1)S(1)}, u32[]{:S(2)}, u32[]{:S(2)}) collective-permute-start(bf16[16,16,128]{2,1,0:T(8,128)(2,1)S(1)} %state.1), channel_id=1, source_target_pairs={{24,0},{25,1},{26,2},{27,3},{28,4},{29,5},{30,6},{31,7}} | collective-permute-start | bytes 196616 | tf_op jit(solution)/shard_map/ppermute | solution.py:445
  10.3 9.4 %collective-permute-start.1 = (bf16[16,16,128]{2,1,0:T(8,128)(2,1)S(1)}, bf16[16,16,128]{2,1,0:T(8,128)(2,1)S(1)}, u32[]{:S(2)}, u32[]{:S(2)}) collective-permute-start(bf16[16,16,128]{2,1,0:T(8,128)(2,1)S(1)} %state.1), channel_id=1, source_target_pairs={{16,0},{24,8},{17,1},{25,9},{18,2},{26,10},{19,3},{27,11},{20,4},{... | collective-permute-start | bytes 196616 | tf_op jit(solution)/shard_map/ppermute | solution.py:445
  11.6 8.2 %collective-permute-start = (bf16[16,16,128]{2,1,0:T(8,128)(2,1)S(1)}, bf16[16,16,128]{2,1,0:T(8,128)(2,1)S(1)}, u32[]{:S(2)}, u32[]{:S(2)}) collective-permute-start(bf16[16,16,128]{2,1,0:T(8,128)(2,1)S(1)} %state.1), channel_id=1, source_target_pairs={{8,0},{16,8},{24,16},{9,1},{17,9},{25,17},{10,2},{18,10},{26,18},{... | collective-permute-start | bytes 196616 | tf_op jit(solution)/shard_map/ppermute | solution.py:445
  14.5 5.4 %copy-start.1 = (bf16[1,2048,128]{2,1,0:T(8,128)(2,1)S(1)}, bf16[1,2048,128]{2,1,0:T(8,128)(2,1)}, u32[]{:S(2)}) copy-start(bf16[1,2048,128]{2,1,0:T(8,128)(2,1)} %param.12) | copy-start | bytes 1572868
  14.5 5.4 %copy-start.2 = (bf16[1,2048,128]{2,1,0:T(8,128)(2,1)S(1)}, bf16[1,2048,128]{2,1,0:T(8,128)(2,1)}, u32[]{:S(2)}) copy-start(bf16[1,2048,128]{2,1,0:T(8,128)(2,1)} %param.11) | copy-start | bytes 1572868
  19.9 2.0 %copy-start.4 = (bf16[2048,128]{1,0:T(8,128)(2,1)S(1)}, bf16[2048,128]{1,0:T(8,128)(2,1)}, u32[]{:S(2)}) copy-start(bf16[2048,128]{1,0:T(8,128)(2,1)} %gate.1.now) | copy-start | bytes 1572868
  19.9 2.0 %copy-start.8 = (bf16[128,128]{1,0:T(8,128)(2,1)S(1)}, bf16[128,128]{1,0:T(8,128)(2,1)}, u32[]{:S(2)}) copy-start(bf16[128,128]{1,0:T(8,128)(2,1)} %filters.3) | copy-start | bytes 98308
  20.6 14.7 %collective-permute-start.4 = (bf16[2048,128]{1,0:T(8,128)(2,1)S(1)}, bf16[2048,128]{1,0:T(8,128)(2,1)S(1)}, u32[]{:S(2)}, u32[]{:S(2)}) collective-permute-start(bf16[2048,128]{1,0:T(8,128)(2,1)S(1)} %get-tuple-element.37.dz1), channel_id=1, source_target_pairs={{8,0},{16,8},{24,16},{9,1},{17,9},{25,17},{10,2},{18,10},{26,18},{... | collective-permute-start | bytes 1572872 | tf_op jit(solution)/shard_map/ppermute | solution.py:445
  28.2 3.2 %collective-permute-start.5 = (bf16[9,16,128]{2,1,0:T(8,128)(2,1)S(1)}, bf16[9,16,128]{2,1,0:T(8,128)(2,1)S(1)}, u32[]{:S(2)}, u32[]{:S(2)}) collective-permute-start(bf16[9,16,128]{2,1,0:T(8,128)(2,1)S(1)} %slice.19), channel_id=1, source_target_pairs={{0,1},{1,0},{2,3},{3,2},{4,5},{5,4},{6,7},{7,6},{8,9},{9,8},{10,11... | collective-permute-start | bytes 110600 | tf_op jit(solution)/shard_map/ppermute | solution.py:450
  31.5 6.2 %collective-permute-start.6 = (bf16[25,16,128]{2,1,0:T(8,128)(2,1)S(1)}, bf16[25,16,128]{2,1,0:T(8,128)(2,1)S(1)}, u32[]{:S(2)}, u32[]{:S(2)}) collective-permute-start(bf16[25,16,128]{2,1,0:T(8,128)(2,1)S(1)} %pad_maximum_fusion), channel_id=1, source_target_pairs={{0,8},{8,0},{16,24},{24,16},{1,9},{9,1},{17,25},{25,17},{2,10},{10... | collective-permute-start | bytes 307208 | tf_op jit(solution)/shard_map/ppermute | solution.py:450
  35.3 5.5 %copy-start.6 = (bf16[1,2048,128]{2,1,0:T(8,128)(2,1)S(1)}, bf16[1,2048,128]{2,1,0:T(8,128)(2,1)}, u32[]{:S(2)}) copy-start(bf16[1,2048,128]{2,1,0:T(8,128)(2,1)} %param.10) | copy-start | bytes 1572868
  36.0 4.8 %copy-start.5 = (bf16[1,2048,128]{2,1,0:T(8,128)(2,1)S(1)}, bf16[1,2048,128]{2,1,0:T(8,128)(2,1)}, u32[]{:S(2)}) copy-start(bf16[1,2048,128]{2,1,0:T(8,128)(2,1)} %param.9) | copy-start | bytes 1572868
  37.8 7.9 %collective-permute-start.7 = (bf16[25,16,128]{2,1,0:T(8,128)(2,1)S(1)}, bf16[25,16,128]{2,1,0:T(8,128)(2,1)S(1)}, u32[]{:S(2)}, u32[]{:S(2)}) collective-permute-start(bf16[25,16,128]{2,1,0:T(8,128)(2,1)S(1)} %pad_maximum_fusion.1), channel_id=1, source_target_pairs={{0,16},{8,24},{16,0},{24,8},{1,17},{9,25},{17,1},{25,9},{2,18},{10... | collective-permute-start | bytes 307208 | tf_op jit(solution)/shard_map/ppermute | solution.py:450

commit v2 on v1

--- a/solution.py
+++ b/solution.py
@@ -347,15 +347,10 @@
     rates = wide_rate[...]
     weights = list(weights)
     for bit in bits:
-        high = (place & bit) != 0
-        passed = TILE * (place & (bit - 1)) + 1
-        reach = jnp.exp(-rates * passed.astype(F32))
-        weights.pop(0)[...] = jnp.where(high, reach, 0.0)
-        if bit != bits[-1]:
-            run = jnp.exp(-rates * (TILE * bit))
-            one = jnp.ones_like(run)
-            weights.pop(0)[...] = jnp.where(high, run, one)
-            weights.pop(0)[...] = jnp.where(high, one, run)
+        low = (place & bit) == 0
+        one = jnp.ones_like(rates)
+        weights.pop(0)[...] = jnp.where(low, one, 0.0)
+        weights.pop(0)[...] = jnp.where(low, jnp.exp(-rates * (2 * TILE * bit)), one)
     mr_turned[...] = nn(filters[...], reversal())
     _, cols = iotas()
     coeffs = residue[...] * jnp.sqrt(one_minus_exp(2.0 * rate[...]))
@@ -558,9 +553,9 @@
         after_shard, rate,
     )
 
-    bits = scan_bits()
+    bits = scan_bits()[::-1]
     few_full = jax.ShapeDtypeStruct((filter_chunks + 1, LANES, TILE), F32)
-    factors = 3 * len(bits) - 2
+    factors = 2 * (len(bits) - 1)
     z2, grad_mr_value, grad_li_key, within_zeros = call(
         within_kernel, "within",
         [wide, table, wide, wide, wide, wide], [wide] * 3 + [whole(few_full)],
@@ -569,7 +564,7 @@
 
     factor_shapes = [few_full, wide_half, table_full] + [chunk_full] * factors
     factor_zeros, after, mr_turned, *weights = call(
-        functools.partial(factor_kernel, bits), "factor",
+        functools.partial(factor_kernel, bits[1:]), "factor",
         [whole(chunk_full), modes, modes, whole(mr_filter), anywhere],
         [whole(leaf) for leaf in factor_shapes], factor_shapes, grid=1,
     )(wide_rate, rate, residue, mr_filter, dz1_later)
@@ -581,22 +576,20 @@
     )(dz1, dz1_later, mr_turned, query, key)
 
     assert lax.axis_size("dp") == 2
-    half = packed[blocks:]
+    state, half = packed[:blocks], packed[blocks:]
+    reached = shifted(state, "seq", bits[0]).astype(F32)
     sums = half.astype(F32) + swapped(half, "dp", 1).astype(F32) + within_zeros
-    packed = jnp.concatenate([packed[:blocks], sums.astype(BF16)], axis=0)
-    zeros = [factor_zeros]
-    before_shard = jnp.zeros(back.shape, F32)
-    for bit in bits:
+    half = sums.astype(BF16)
+    partner = swapped(half, "seq", bits[0])
+    zeros = factor_zeros
+    for bit in bits[1:]:
+        sums = half.astype(F32) + partner.astype(F32) + zeros
+        sent = weights.pop(0) * state.astype(F32) + weights.pop(0) * reached
+        packed = jnp.concatenate([sent.astype(BF16), sums.astype(BF16)], axis=0)
         other = swapped(packed, "seq", bit)
-        mine, theirs = packed[:blocks].astype(F32), other[:blocks].astype(F32)
-        before_shard = before_shard + weights.pop(0) * theirs
+        reached = other[:blocks].astype(F32) + jnp.exp(-TILE * bit * wide_rate) * reached
         half, partner = packed[blocks:], other[blocks:]
-        if bit != bits[-1]:
-            sums = half.astype(F32) + partner.astype(F32)
-            if zeros:
-                sums = sums + zeros.pop(0)
-            total = weights.pop(0) * theirs + weights.pop(0) * mine
-            packed = jnp.concatenate([total.astype(BF16), sums.astype(BF16)], axis=0)
+    before_shard = reached * jnp.exp(-wide_rate)
     residue_full = jax.ShapeDtypeStruct((LANES, TILE), F32)
     grad_li_value, grad_filter, grad_residue = call(
         value_kernel, "value",

time: 47.8 us -> 47.7 us (level)
  waiting for transfers between devices: 7.5 us -> 4.26 us
  starting transfers between devices: 15.9 us -> 19 us
    ppermute x3, waiting for transfers between devices: 3.41 us -> 0.01 us  [swapped(): lax.ppermute(value, axis, [(source, source ^ bit) for source in range(cou...]
    ppermute x5 -> x6, starting transfers between devices: 10.1 us -> 12.1 us  [shifted(): lax.ppermute(value, axis, [(source, source + steps) for source in range(f...]
    ppermute x3, starting transfers between devices: 5.78 us -> 6.92 us  [swapped(): lax.ppermute(value, axis, [(source, source ^ bit) for source in range(cou...]
    ppermute x5 -> x6, waiting for transfers between devices: 4.09 us -> 4.26 us  [shifted(): lax.ppermute(value, axis, [(source, source + steps) for source in range(f...]
  transfers between devices with their start and end apart: 8 -> 9, of which waited for: 5 -> 3; matrix products, arithmetic and copies ran while one was open for 0% -> 0% of each run, Pallas kernels for 39% -> 39%
where the time goes in v2:
time: 47.7 us; the launch traced here: 47.4 us
  Pallas kernels  23 us (48%)
  starting transfers between devices  19 us (40%)
  waiting for transfers between devices  4.26 us (9%)
  between operations  0.94 us (2%)
    ppermute x6, starting transfers between devices, shifted(): lax.ppermute(value, axis, [(source, source + steps) for source in range(f...  12.1 us
    ppermute x3, starting transfers between devices, swapped(): lax.ppermute(value, axis, [(source, source ^ bit) for source in range(cou...  6.92 us
    pallas_call x1, Pallas kernels, per_device(): call(forward_kernel, 'forward', [twice(spec) for spec in [wide, wide, tab...  6.34 us
    ppermute x6, waiting for transfers between devices, shifted(): lax.ppermute(value, axis, [(source, source + steps) for source in range(f...  4.26 us
    pallas_call x1, Pallas kernels, per_device(): call(product_kernel, 'product', [twice(spec) for spec in (wide, wide, tab...  3.27 us
    pallas_call x1, Pallas kernels, per_device(): call(within_kernel, 'within', [wide, table, wide, wide, wide, wide], [wid...  3.1 us
    pallas_call x1, Pallas kernels, per_device(): call(local_kernel, 'local', [wide, wide, table], [wide], [wide_full])  2.26 us
    pallas_call x1, Pallas kernels, per_device(): call(gate_kernel, 'gate', [distant] * 2, [distant], [wide_half], [pltpu.V...  2.17 us
  transfers between devices with their start and end apart: 9, of which 3 were waited for; matrix products, arithmetic and copies ran while one was open for 0% of the time, Pallas kernels for 39%

profile of v2, /device:TPU:0, one launch (start us, length us, event | category | flops | bytes accessed | tf_op | source)
XLA Modules:
  0.0 47.4 jit_solution(3674987591816069963)
XLA Ops:
  0.6 0.0 copy-start
  0.6 0.0 copy-start.3
  0.7 0.0 copy-start.7
  0.7 2.2 %gate.1.now = bf16[2048,128]{1,0:T(8,128)(2,1)} custom-call(bf16[2048,128]{1,0:T(8,128)(2,1)} %bitcast.27, bf16[2048,128]{1,0:T(8,128)(2,1)} %bitcast.29), custom_call_target="tpu_custom_call" | custom-call | bytes 1 | tf_op jit(solution)/shard_map/gate/pallas_call | solution.py:508
  2.8 5.0 %collective-permute-start.3 = (bf16[2048,128]{1,0:T(8,128)(2,1)}, bf16[2048,128]{1,0:T(8,128)(2,1)S(1)}, u32[]{:S(2)}, u32[]{:S(2)}) collective-permute-start(bf16[2048,128]{1,0:T(8,128)(2,1)} %gate.1.now), channel_id=1, source_target_pairs={{0,8},{8,16},{16,24},{1,9},{9,17},{17,25},{2,10},{10,18},{18,26},{... | collective-permute-start | bytes 1572872 | tf_op jit(solution)/shard_map/ppermute | solution.py:440
  7.8 0.0 copy-done
  7.8 0.0 copy-done.3
  7.8 0.0 copy-done.7
  7.8 0.0 copy-start.9
  7.8 1.2 %state.1 = bf16[16,16,128]{2,1,0:T(8,128)(2,1)S(1)} custom-call(bf16[2048,128]{1,0:T(8,128)(2,1)S(1)} %bitcast.14, bf16[2048,128]{1,0:T(8,128)(2,1)S(1)} %bitcast.24, f32[16,128]{1,0:T(8,128)S(1)} %bitcast.31), custom_call_target="tpu_custom_call" | custom-call | bytes 1 | tf_op jit(solution)/shard_map/state/pallas_call | solution.py:518
  9.0 1.3 %collective-permute-start.2 = (bf16[16,16,128]{2,1,0:T(8,128)(2,1)S(1)}, bf16[16,16,128]{2,1,0:T(8,128)(2,1)S(1)}, u32[]{:S(2)}, u32[]{:S(2)}) collective-permute-start(bf16[16,16,128]{2,1,0:T(8,128)(2,1)S(1)} %state.1), channel_id=1, source_target_pairs={{24,0},{25,1},{26,2},{27,3},{28,4},{29,5},{30,6},{31,7}} | collective-permute-start | bytes 196616 | tf_op jit(solution)/shard_map/ppermute | solution.py:440
  10.3 1.3 %collective-permute-start.1 = (bf16[16,16,128]{2,1,0:T(8,128)(2,1)S(1)}, bf16[16,16,128]{2,1,0:T(8,128)(2,1)S(1)}, u32[]{:S(2)}, u32[]{:S(2)}) collective-permute-start(bf16[16,16,128]{2,1,0:T(8,128)(2,1)S(1)} %state.1), channel_id=1, source_target_pairs={{16,0},{24,8},{17,1},{25,9},{18,2},{26,10},{19,3},{27,11},{20,4},{... | collective-permute-start | bytes 196616 | tf_op jit(solution)/shard_map/ppermute | solution.py:440
  11.6 1.3 %collective-permute-start = (bf16[16,16,128]{2,1,0:T(8,128)(2,1)S(1)}, bf16[16,16,128]{2,1,0:T(8,128)(2,1)S(1)}, u32[]{:S(2)}, u32[]{:S(2)}) collective-permute-start(bf16[16,16,128]{2,1,0:T(8,128)(2,1)S(1)} %state.1), channel_id=1, source_target_pairs={{8,0},{16,8},{24,16},{9,1},{17,9},{25,17},{10,2},{18,10},{26,18},{... | collective-permute-start | bytes 196616 | tf_op jit(solution)/shard_map/ppermute | solution.py:440
  12.9 0.0 copy-done.9
  12.9 1.6 %table.1 = (bf16[2048,128]{1,0:T(8,128)(2,1)S(1)}, bf16[2048,128]{1,0:T(8,128)(2,1)S(1)}, bf16[2048,128]{1,0:T(8,128)(2,1)S(1)}, f32[128,128]{1,0:T(8,128)S(1)},...) custom-call(f32[16,128]{1,0:T(8,128)S(1)} %bitcast.32, f32[16,128]{1,0:T(8,128)S(1)} %bitcast.35), custom_call_target="tpu_custom_call" | custom-call | bytes 1 | tf_op jit(solution)/shard_map/table/pallas_call | solution.py:523
  14.5 2.3 %local.1 = f32[2048,128]{1,0:T(8,128)S(1)} custom-call(bf16[2048,128]{1,0:T(8,128)(2,1)S(1)} %bitcast.15, bf16[2048,128]{1,0:T(8,128)(2,1)S(1)} %bitcast.25, f32[128,128]{1,0:T(8,128)S(1)} %get-tuple-element.33.turned), custom_call_target="tpu_custom_call" | custom-call | bytes 1 | tf_op jit(solution)/shard_map/local/pallas_call | solution.py:527
  16.8 0.9 %collective-permute-done.2 = bf16[16,16,128]{2,1,0:T(8,128)(2,1)S(1)} collective-permute-done((bf16[16,16,128]{2,1,0:T(8,128)(2,1)S(1)}, bf16[16,16,128]{2,1,0:T(8,128)(2,1)S(1)}, u32[]{:S(2)}, u32[]{:S(2)}) %collective-permute-start.2) | collective-permute-done | bytes 65568 | tf_op jit(solution)/shard_map/ppermute | solution.py:440
  17.7 2.1 %collective-permute-done.1 = bf16[16,16,128]{2,1,0:T(8,128)(2,1)S(1)} collective-permute-done((bf16[16,16,128]{2,1,0:T(8,128)(2,1)S(1)}, bf16[16,16,128]{2,1,0:T(8,128)(2,1)S(1)}, u32[]{:S(2)}, u32[]{:S(2)}) %collective-permute-start.1) | collective-permute-done | bytes 65568 | tf_op jit(solution)/shard_map/ppermute | solution.py:440
  19.8 0.0 collective-permute-done
  19.8 0.1 add_multiply_fusion.states.after_shard
  19.8 0.0 collective-permute-done.3.before
  19.8 0.0 copy-done.1
  19.9 0.0 copy-done.2
  19.9 0.0 copy-start.4
  19.9 0.0 copy-start.8
  19.9 0.7 %middle.1 = (bf16[2048,128]{1,0:T(8,128)(2,1)S(1)}, f32[2048,128]{1,0:T(8,128)S(1)}) custom-call(f32[16,16,128]{2,1,0:T(8,128)S(1)} %add_multiply_fusion.states.after_shard, f32[2048,128]{1,0:T(8,128)S(1)} %local.1, bf16[2048,128]{1,0:T(8,128)(2,1)S(1)} %get-tuple-element.34.to_next, bf16[2048,128]{1,0:T(8,128)(2,1)S(1)} %bitcast.18, ...), custom_call_target="tpu_custom_call" | custom-call | bytes 1 | tf_op jit(solution)/shard_map/middle/pallas_call | solution.py:536
  20.6 1.3 %collective-permute-start.4 = (bf16[2048,128]{1,0:T(8,128)(2,1)S(1)}, bf16[2048,128]{1,0:T(8,128)(2,1)S(1)}, u32[]{:S(2)}, u32[]{:S(2)}) collective-permute-start(bf16[2048,128]{1,0:T(8,128)(2,1)S(1)} %get-tuple-element.35.dz1), channel_id=1, source_target_pairs={{8,0},{16,8},{24,16},{9,1},{17,9},{25,17},{10,2},{18,10},{26,18},{... | collective-permute-start | bytes 1572872 | tf_op jit(solution)/shard_map/ppermute | solution.py:440
  21.9 0.0 copy-done.4
  21.9 0.0 copy-done.8
  21.9 6.3 %forward.1 = (f32[2048,128]{1,0:T(8,128)S(1)}, bf16[2048,128]{1,0:T(8,128)(2,1)S(1)}, bf16[25,16,128]{2,1,0:T(8,128)(2,1)S(1)}) custom-call(bf16[2048,128]{1,0:T(8,128)(2,1)S(1)} %collective-permute-done.3.before, bf16[2048,128]{1,0:T(8,128)(2,1)S(1)} %copy-done.4, bf16[128,128]{1,0:T(8,128)(2,1)S(1)} %copy-done.8, bf16[2048,128]{1,0:T(8,128)(2,1)S(1)} %bitcast.22, ...), custom_call_target="tpu_custom_call" | custom-call | bytes 1 | tf_op jit(solution)/shard_map/forward/pallas_call | solution.py:545
  28.3 0.1 collective-permute-start.6
  28.3 3.1 %within.1 = (f32[2048,128]{1,0:T(8,128)S(1)}, bf16[2048,128]{1,0:T(8,128)(2,1)}, bf16[2048,128]{1,0:T(8,128)(2,1)}, f32[9,16,128]{2,1,0:T(8,128)S(1)}) custom-call(bf16[2048,128]{1,0:T(8,128)(2,1)S(1)} %get-tuple-element.41.u2, f32[128,128]{1,0:T(8,128)S(1)} %get-tuple-element.42.taps, f32[2048,128]{1,0:T(8,128)S(1)} %get-tuple-element.43.z1, ...), custom_call_target="tpu_custom_call" | custom-call | bytes 1 | tf_op jit(solution)/shard_map/within/pallas_call | solution.py:559
  31.4 0.0 collective-permute-done.6
  31.5 3.9 %collective-permute-start.7 = (bf16[9,16,128]{2,1,0:T(8,128)(2,1)S(1)}, bf16[9,16,128]{2,1,0:T(8,128)(2,1)S(1)}, u32[]{:S(2)}, u32[]{:S(2)}) collective-permute-start(bf16[9,16,128]{2,1,0:T(8,128)(2,1)S(1)} %add_convert_fusion.1), channel_id=1, source_target_pairs={{0,16},{8,24},{16,0},{24,8},{1,17},{9,25},{17,1},{25,9},{2,18},{10... | collective-permute-start | bytes 110600 | tf_op jit(solution)/shard_map/ppermute | solution.py:445
  35.4 1.9 %collective-permute-start.5 = (bf16[16,16,128]{2,1,0:T(8,128)(2,1)S(1)}, bf16[16,16,128]{2,1,0:T(8,128)(2,1)S(1)}, u32[]{:S(2)}, u32[]{:S(2)}) collective-permute-start(bf16[16,16,128]{2,1,0:T(8,128)(2,1)S(1)} %slice.12), channel_id=1, source_target_pairs={{0,16},{8,24},{1,17},{9,25},{2,18},{10,26},{3,19},{11,27},{4,20},{... | collective-permute-start | bytes 196616 | tf_op jit(solution)/shard_map/ppermute | solution.py:440
  37.3 0.0 collective-permute-done.4.later
  37.3 0.0 copy-start.6
  37.3 0.6 %factor.1 = (f32[9,16,128]{2,1,0:T(8,128)S(1)}, bf16[2048,128]{1,0:T(8,128)(2,1)S(1)}, f32[128,128]{1,0:T(8,128)S(1)}, f32[16,16,128]{2,1,0:T(8,128)S(1)}, f32[16,16,128]{2,1,0:T(8,128)S(1)}) custom-call(f32[16,16,128]{2,1,0:T(8,128)S(1)} %get-tuple-element.32.wide_rate, f32[16,128]{1,0:T(8,128)S(1)} %bitcast.34, f32[16,128]{1,0:T(8,128)S(1)} %bitcast.36, ...), custom_call_target="tpu_custom_call" | custom-call | bytes 1 | tf_op jit(solution)/shard_map/factor/pallas_call | solution.py:566
  38.0 0.0 copy-start.5
  38.0 0.0 collective-permute-done.7
  38.0 1.2 %collective-permute-done.5 = bf16[16,16,128]{2,1,0:T(8,128)(2,1)S(1)} collective-permute-done((bf16[16,16,128]{2,1,0:T(8,128)(2,1)S(1)}, bf16[16,16,128]{2,1,0:T(8,128)(2,1)S(1)}, u32[]{:S(2)}, u32[]{:S(2)}) %collective-permute-start.5) | collective-permute-done | bytes 65568 | tf_op jit(solution)/shard_map/ppermute | solution.py:440
  39.3 3.0 %collective-permute-start.8 = (bf16[25,16,128]{2,1,0:T(8,128)(2,1)S(1)}, bf16[25,16,128]{2,1,0:T(8,128)(2,1)S(1)}, u32[]{:S(2)}, u32[]{:S(2)}) collective-permute-start(bf16[25,16,128]{2,1,0:T(8,128)(2,1)S(1)} %pad_maximum_fusion), channel_id=1, source_target_pairs={{0,8},{8,0},{16,24},{24,16},{1,9},{9,1},{17,25},{25,17},{2,10},{10... | collective-permute-start | bytes 307208 | tf_op jit(solution)/shard_map/ppermute | solution.py:445
  42.3 0.0 copy-done.6
  42.3 0.0 copy-done.5
  42.3 3.3 %product.1 = (bf16[2048,128]{1,0:T(8,128)(2,1)}, bf16[2048,128]{1,0:T(8,128)(2,1)}) custom-call(bf16[2048,128]{1,0:T(8,128)(2,1)S(1)} %get-tuple-element.35.dz1, bf16[2048,128]{1,0:T(8,128)(2,1)S(1)} %collective-permute-done.4.later, f32[128,128]{1,0:T(8,128)S(1)} %get-tuple-element.36.turned, bf16[2048,128]{1,0:T(8,128)(2,1)S(1)} %bitcast.28, ...), custom_call_target="tpu_custom_call" | custom-call | bytes 1 | tf_op jit(solution)/shard_map/product/pallas_call | solution.py:572
  45.6 0.0 collective-permute-done.8
  45.6 0.1 fusion.3.states
  45.6 1.8 %value.1 = (bf16[2048,128]{1,0:T(8,128)(2,1)}, f32[128,128]{1,0:T(8,128)}, f32[16,128]{1,0:T(8,128)}) custom-call(f32[16,16,128]{2,1,0:T(8,128)S(1)} %fusion.3.states, bf16[2048,128]{1,0:T(8,128)(2,1)S(1)} %get-tuple-element.52.after, f32[2048,128]{1,0:T(8,128)S(1)} %get-tuple-element.53.z2, bf16[2048,128]{1,0:T(8,128)(2,1)S(1)} %bitcast.17, ...), custom_call_target="tpu_custom_call" | custom-call | bytes 1 | tf_op jit(solution)/shard_map/value/pallas_call | solution.py:594
  (9 shorter events, 0.1 us)
Async XLA Ops:
  0.6 7.2 %copy-start = (bf16[1,2048,128]{2,1,0:T(8,128)(2,1)S(1)}, bf16[1,2048,128]{2,1,0:T(8,128)(2,1)}, u32[]{:S(2)}) copy-start(bf16[1,2048,128]{2,1,0:T(8,128)(2,1)} %param.14) | copy-start | bytes 1572868
  0.6 7.2 %copy-start.3 = (bf16[1,2048,128]{2,1,0:T(8,128)(2,1)S(1)}, bf16[1,2048,128]{2,1,0:T(8,128)(2,1)}, u32[]{:S(2)}) copy-start(bf16[1,2048,128]{2,1,0:T(8,128)(2,1)} %param.13) | copy-start | bytes 1572868
  0.7 7.2 %copy-start.7 = (f32[128,16]{0,1:T(8,128)S(1)}, f32[128,16]{0,1:T(8,128)}, u32[]{:S(2)}) copy-start(f32[128,16]{0,1:T(8,128)} %param.17) | copy-start | bytes 24580
  2.8 17.0 %collective-permute-start.3 = (bf16[2048,128]{1,0:T(8,128)(2,1)}, bf16[2048,128]{1,0:T(8,128)(2,1)S(1)}, u32[]{:S(2)}, u32[]{:S(2)}) collective-permute-start(bf16[2048,128]{1,0:T(8,128)(2,1)} %gate.1.now), channel_id=1, source_target_pairs={{0,8},{8,16},{16,24},{1,9},{9,17},{17,25},{2,10},{10,18},{18,26},{... | collective-permute-start | bytes 1572872 | tf_op jit(solution)/shard_map/ppermute | solution.py:440
  7.8 5.1 %copy-start.9 = (f32[128,16]{0,1:T(8,128)S(1)}, f32[128,16]{0,1:T(8,128)}, u32[]{:S(2)}) copy-start(f32[128,16]{0,1:T(8,128)} %param.16) | copy-start | bytes 24580
  9.0 8.7 %collective-permute-start.2 = (bf16[16,16,128]{2,1,0:T(8,128)(2,1)S(1)}, bf16[16,16,128]{2,1,0:T(8,128)(2,1)S(1)}, u32[]{:S(2)}, u32[]{:S(2)}) collective-permute-start(bf16[16,16,128]{2,1,0:T(8,128)(2,1)S(1)} %state.1), channel_id=1, source_target_pairs={{24,0},{25,1},{26,2},{27,3},{28,4},{29,5},{30,6},{31,7}} | collective-permute-start | bytes 196616 | tf_op jit(solution)/shard_map/ppermute | solution.py:440
  10.3 9.4 %collective-permute-start.1 = (bf16[16,16,128]{2,1,0:T(8,128)(2,1)S(1)}, bf16[16,16,128]{2,1,0:T(8,128)(2,1)S(1)}, u32[]{:S(2)}, u32[]{:S(2)}) collective-permute-start(bf16[16,16,128]{2,1,0:T(8,128)(2,1)S(1)} %state.1), channel_id=1, source_target_pairs={{16,0},{24,8},{17,1},{25,9},{18,2},{26,10},{19,3},{27,11},{20,4},{... | collective-permute-start | bytes 196616 | tf_op jit(solution)/shard_map/ppermute | solution.py:440
  11.6 8.2 %collective-permute-start = (bf16[16,16,128]{2,1,0:T(8,128)(2,1)S(1)}, bf16[16,16,128]{2,1,0:T(8,128)(2,1)S(1)}, u32[]{:S(2)}, u32[]{:S(2)}) collective-permute-start(bf16[16,16,128]{2,1,0:T(8,128)(2,1)S(1)} %state.1), channel_id=1, source_target_pairs={{8,0},{16,8},{24,16},{9,1},{17,9},{25,17},{10,2},{18,10},{26,18},{... | collective-permute-start | bytes 196616 | tf_op jit(solution)/shard_map/ppermute | solution.py:440
  14.5 5.4 %copy-start.1 = (bf16[1,2048,128]{2,1,0:T(8,128)(2,1)S(1)}, bf16[1,2048,128]{2,1,0:T(8,128)(2,1)}, u32[]{:S(2)}) copy-start(bf16[1,2048,128]{2,1,0:T(8,128)(2,1)} %param.12) | copy-start | bytes 1572868
  14.5 5.4 %copy-start.2 = (bf16[1,2048,128]{2,1,0:T(8,128)(2,1)S(1)}, bf16[1,2048,128]{2,1,0:T(8,128)(2,1)}, u32[]{:S(2)}) copy-start(bf16[1,2048,128]{2,1,0:T(8,128)(2,1)} %param.11) | copy-start | bytes 1572868
  19.9 2.0 %copy-start.4 = (bf16[2048,128]{1,0:T(8,128)(2,1)S(1)}, bf16[2048,128]{1,0:T(8,128)(2,1)}, u32[]{:S(2)}) copy-start(bf16[2048,128]{1,0:T(8,128)(2,1)} %gate.1.now) | copy-start | bytes 1572868
  19.9 2.0 %copy-start.8 = (bf16[128,128]{1,0:T(8,128)(2,1)S(1)}, bf16[128,128]{1,0:T(8,128)(2,1)}, u32[]{:S(2)}) copy-start(bf16[128,128]{1,0:T(8,128)(2,1)} %filters.3) | copy-start | bytes 98308
  20.6 16.7 %collective-permute-start.4 = (bf16[2048,128]{1,0:T(8,128)(2,1)S(1)}, bf16[2048,128]{1,0:T(8,128)(2,1)S(1)}, u32[]{:S(2)}, u32[]{:S(2)}) collective-permute-start(bf16[2048,128]{1,0:T(8,128)(2,1)S(1)} %get-tuple-element.35.dz1), channel_id=1, source_target_pairs={{8,0},{16,8},{24,16},{9,1},{17,9},{25,17},{10,2},{18,10},{26,18},{... | collective-permute-start | bytes 1572872 | tf_op jit(solution)/shard_map/ppermute | solution.py:440
  28.3 3.2 %collective-permute-start.6 = (bf16[9,16,128]{2,1,0:T(8,128)(2,1)S(1)}, bf16[9,16,128]{2,1,0:T(8,128)(2,1)S(1)}, u32[]{:S(2)}, u32[]{:S(2)}) collective-permute-start(bf16[9,16,128]{2,1,0:T(8,128)(2,1)S(1)} %slice.13), channel_id=1, source_target_pairs={{0,1},{1,0},{2,3},{3,2},{4,5},{5,4},{6,7},{7,6},{8,9},{9,8},{10,11... | collective-permute-start | bytes 110600 | tf_op jit(solution)/shard_map/ppermute | solution.py:445
  31.5 6.5 %collective-permute-start.7 = (bf16[9,16,128]{2,1,0:T(8,128)(2,1)S(1)}, bf16[9,16,128]{2,1,0:T(8,128)(2,1)S(1)}, u32[]{:S(2)}, u32[]{:S(2)}) collective-permute-start(bf16[9,16,128]{2,1,0:T(8,128)(2,1)S(1)} %add_convert_fusion.1), channel_id=1, source_target_pairs={{0,16},{8,24},{16,0},{24,8},{1,17},{9,25},{17,1},{25,9},{2,18},{10... | collective-permute-start | bytes 110600 | tf_op jit(solution)/shard_map/ppermute | solution.py:445
  35.4 3.9 %collective-permute-start.5 = (bf16[16,16,128]{2,1,0:T(8,128)(2,1)S(1)}, bf16[16,16,128]{2,1,0:T(8,128)(2,1)S(1)}, u32[]{:S(2)}, u32[]{:S(2)}) collective-permute-start(bf16[16,16,128]{2,1,0:T(8,128)(2,1)S(1)} %slice.12), channel_id=1, source_target_pairs={{0,16},{8,24},{1,17},{9,25},{2,18},{10,26},{3,19},{11,27},{4,20},{... | collective-permute-start | bytes 196616 | tf_op jit(solution)/shard_map/ppermute | solution.py:440
  37.3 5.0 %copy-start.6 = (bf16[1,2048,128]{2,1,0:T(8,128)(2,1)S(1)}, bf16[1,2048,128]{2,1,0:T(8,128)(2,1)}, u32[]{:S(2)}) copy-start(bf16[1,2048,128]{2,1,0:T(8,128)(2,1)} %param.10) | copy-start | bytes 1572868
  38.0 4.3 %copy-start.5 = (bf16[1,2048,128]{2,1,0:T(8,128)(2,1)S(1)}, bf16[1,2048,128]{2,1,0:T(8,128)(2,1)}, u32[]{:S(2)}) copy-start(bf16[1,2048,128]{2,1,0:T(8,128)(2,1)} %param.9) | copy-start | bytes 1572868
  39.3 6.2 %collective-permute-start.8 = (bf16[25,16,128]{2,1,0:T(8,128)(2,1)S(1)}, bf16[25,16,128]{2,1,0:T(8,128)(2,1)S(1)}, u32[]{:S(2)}, u32[]{:S(2)}) collective-permute-start(bf16[25,16,128]{2,1,0:T(8,128)(2,1)S(1)} %pad_maximum_fusion), channel_id=1, source_target_pairs={{0,8},{8,0},{16,24},{24,16},{1,9},{9,1},{17,25},{25,17},{2,10},{10... | collective-permute-start | bytes 307208 | tf_op jit(solution)/shard_map/ppermute | solution.py:445

commit v3 on v2

--- a/solution.py
+++ b/solution.py
@@ -377,7 +377,10 @@
         grad_value[span, :] = (du2_here * li_key[span, :].astype(F32) * z1_here).astype(BF16)
 
 
-def product_kernel(dz1, later, turned, query, key, grad_query, grad_key):
+def product_kernel(part, dz1, later, turned, query, key, *refs):
+    grad_query, grad_key = refs[2 * part : 2 * part + 2]
+    if part == 0:
+        refs[2][...] = jnp.zeros_like(refs[2])
     rows, cols = iotas()
     lower = ones_where(rows >= cols)
     lower_half = beside(lower, lower)
@@ -484,7 +487,7 @@
     chunk_half = jax.ShapeDtypeStruct((blocks, LANES, TILE), BF16)
     chunk_full = jax.ShapeDtypeStruct((blocks, LANES, TILE), F32)
 
-    def call(kernel, name, in_specs, out_specs, out_shape, scratch=(), grid=STEPS, limit=VMEM_LIMIT, work=0):
+    def call(kernel, name, in_specs, out_specs, out_shape, scratch=(), grid=STEPS, limit=VMEM_LIMIT, aliases={}):
         return pl.pallas_call(
             kernel,
             grid=(grid,),
@@ -492,10 +495,9 @@
             out_specs=out_specs,
             out_shape=out_shape,
             scratch_shapes=scratch,
+            input_output_aliases=aliases,
             name=name,
-            cost_estimate=pl.CostEstimate(
-                flops=2 * work * channels * TILE * TILE, bytes_accessed=1, transcendentals=0
-            ),
+            cost_estimate=pl.CostEstimate(flops=1, bytes_accessed=1, transcendentals=0),
             compiler_params=pltpu.CompilerParams(vmem_limit_bytes=limit),
         )
 
@@ -569,11 +571,22 @@
         [whole(leaf) for leaf in factor_shapes], factor_shapes, grid=1,
     )(wide_rate, rate, residue, mr_filter, dz1_later)
 
-    grad_query, grad_key = call(
-        product_kernel, "product",
-        [twice(spec) for spec in (wide, wide, table, wide, wide)],
-        [twice(wide), twice(wide)], [wide_half, wide_half], grid=STEPS // 2,
-    )(dz1, dz1_later, mr_turned, query, key)
+    def half_product(part, *made):
+        def half_of(spec):
+            shape = (spec.block_shape[0] * STEPS // 2,) + spec.block_shape[1:]
+            return pl.BlockSpec(shape, lambda i: (part, 0))
+
+        streams = [half_of(spec) for spec in (wide, wide, table, wide, wide)]
+        return call(
+            functools.partial(product_kernel, part), "product",
+            streams + [anywhere] * len(made),
+            [half_of(wide)] * 2 + [whole(few_full)] * (1 - part),
+            [wide_half] * 2 + [few_full] * (1 - part), grid=1,
+            aliases={len(streams) + at: at for at in range(len(made))},
+        )(dz1, dz1_later, mr_turned, query, key, *made)
+
+    *products, product_zeros = half_product(0)
+    grad_query, grad_key = half_product(1, *products)
 
     assert lax.axis_size("dp") == 2
     state, half = packed[:blocks], packed[blocks:]
@@ -581,7 +594,7 @@
     sums = half.astype(F32) + swapped(half, "dp", 1).astype(F32) + within_zeros
     half = sums.astype(BF16)
     partner = swapped(half, "seq", bits[0])
-    zeros = factor_zeros
+    zeros = factor_zeros + product_zeros
     for bit in bits[1:]:
         sums = half.astype(F32) + partner.astype(F32) + zeros
         sent = weights.pop(0) * state.astype(F32) + weights.pop(0) * reached

time: 47.7 us -> 49.5 us (1.038)
  waiting for transfers between devices: 4.26 us -> 6.6 us
  starting transfers between devices: 19 us -> 17.3 us
  Pallas kernels: 23 us -> 23.7 us
    ppermute x3, starting transfers between devices: 6.92 us -> 1.42 us  [swapped(): lax.ppermute(value, axis, [(source, source ^ bit) for source in range(cou...]
    ppermute x6, starting transfers between devices: 12.1 us -> 15.9 us  [shifted(): lax.ppermute(value, axis, [(source, source + steps) for source in range(f...]
    ppermute x3, waiting for transfers between devices: 0.01 us -> 3.58 us  [swapped(): lax.ppermute(value, axis, [(source, source ^ bit) for source in range(cou...]
    ppermute x6, waiting for transfers between devices: 4.26 us -> 3.02 us  [shifted(): lax.ppermute(value, axis, [(source, source + steps) for source in range(f...]
    pallas_call x1 -> x2, Pallas kernels: 3.27 us -> 4.01 us  [half_product(): call(functools.partial(product_kernel, part), 'product', streams + [anywh...]
  transfers between devices with their start and end apart: 9 -> 9, of which waited for: 3 -> 4; matrix products, arithmetic and copies ran while one was open for 0% -> 0% of each run, Pallas kernels for 39% -> 39%
where the time goes in v3:
time: 49.5 us; the launch traced here: 49.2 us
  Pallas kernels  23.7 us (48%)
  starting transfers between devices  17.3 us (35%)
  waiting for transfers between devices  6.6 us (13%)
  between operations  0.95 us (2%)
    ppermute x6, starting transfers between devices, shifted(): lax.ppermute(value, axis, [(source, source + steps) for source in range(f...  15.9 us
    pallas_call x1, Pallas kernels, per_device(): call(forward_kernel, 'forward', [twice(spec) for spec in [wide, wide, tab...  6.33 us
    pallas_call x2, Pallas kernels, half_product(): call(functools.partial(product_kernel, part), 'product', streams + [anywh...  4.01 us
    ppermute x3, waiting for transfers between devices, swapped(): lax.ppermute(value, axis, [(source, source ^ bit) for source in range(cou...  3.58 us
    pallas_call x1, Pallas kernels, per_device(): call(within_kernel, 'within', [wide, table, wide, wide, wide, wide], [wid...  3.1 us
    ppermute x6, waiting for transfers between devices, shifted(): lax.ppermute(value, axis, [(source, source + steps) for source in range(f...  3.02 us
    pallas_call x1, Pallas kernels, per_device(): call(local_kernel, 'local', [wide, wide, table], [wide], [wide_full])  2.26 us
    pallas_call x1, Pallas kernels, per_device(): call(gate_kernel, 'gate', [distant] * 2, [distant], [wide_half], [pltpu.V...  2.17 us
  transfers between devices with their start and end apart: 9, of which 4 were waited for; matrix products, arithmetic and copies ran while one was open for 0% of the time, Pallas kernels for 39%

profile of v3, /device:TPU:0, one launch (start us, length us, event | category | flops | bytes accessed | tf_op | source)
XLA Modules:
  0.0 49.2 jit_solution(9904988687787278478)
XLA Ops:
  0.6 0.0 copy-start
  0.6 0.0 copy-start.5
  0.7 0.0 copy-start.7
  0.7 2.2 %gate.1.now = bf16[2048,128]{1,0:T(8,128)(2,1)} custom-call(bf16[2048,128]{1,0:T(8,128)(2,1)} %bitcast.24, bf16[2048,128]{1,0:T(8,128)(2,1)} %bitcast.27), custom_call_target="tpu_custom_call" | custom-call | flops 1 | bytes 1 | tf_op jit(solution)/shard_map/gate/pallas_call | solution.py:510
  2.8 5.0 %collective-permute-start.3 = (bf16[2048,128]{1,0:T(8,128)(2,1)}, bf16[2048,128]{1,0:T(8,128)(2,1)S(1)}, u32[]{:S(2)}, u32[]{:S(2)}) collective-permute-start(bf16[2048,128]{1,0:T(8,128)(2,1)} %gate.1.now), channel_id=1, source_target_pairs={{0,8},{8,16},{16,24},{1,9},{9,17},{17,25},{2,10},{10,18},{18,26},{... | collective-permute-start | bytes 1572872 | tf_op jit(solution)/shard_map/ppermute | solution.py:443
  7.8 0.0 copy-done
  7.8 0.0 copy-done.5
  7.8 0.0 copy-done.7
  7.8 0.0 copy-start.9
  7.8 1.2 %state.1 = bf16[16,16,128]{2,1,0:T(8,128)(2,1)S(1)} custom-call(bf16[2048,128]{1,0:T(8,128)(2,1)S(1)} %bitcast.14, bf16[2048,128]{1,0:T(8,128)(2,1)S(1)} %bitcast.30, f32[16,128]{1,0:T(8,128)S(1)} %bitcast.33), custom_call_target="tpu_custom_call" | custom-call | flops 1 | bytes 1 | tf_op jit(solution)/shard_map/state/pallas_call | solution.py:520
  9.0 1.3 %collective-permute-start.2 = (bf16[16,16,128]{2,1,0:T(8,128)(2,1)S(1)}, bf16[16,16,128]{2,1,0:T(8,128)(2,1)S(1)}, u32[]{:S(2)}, u32[]{:S(2)}) collective-permute-start(bf16[16,16,128]{2,1,0:T(8,128)(2,1)S(1)} %state.1), channel_id=1, source_target_pairs={{24,0},{25,1},{26,2},{27,3},{28,4},{29,5},{30,6},{31,7}} | collective-permute-start | bytes 196616 | tf_op jit(solution)/shard_map/ppermute | solution.py:443
  10.3 1.3 %collective-permute-start.1 = (bf16[16,16,128]{2,1,0:T(8,128)(2,1)S(1)}, bf16[16,16,128]{2,1,0:T(8,128)(2,1)S(1)}, u32[]{:S(2)}, u32[]{:S(2)}) collective-permute-start(bf16[16,16,128]{2,1,0:T(8,128)(2,1)S(1)} %state.1), channel_id=1, source_target_pairs={{16,0},{24,8},{17,1},{25,9},{18,2},{26,10},{19,3},{27,11},{20,4},{... | collective-permute-start | bytes 196616 | tf_op jit(solution)/shard_map/ppermute | solution.py:443
  11.6 1.3 %collective-permute-start = (bf16[16,16,128]{2,1,0:T(8,128)(2,1)S(1)}, bf16[16,16,128]{2,1,0:T(8,128)(2,1)S(1)}, u32[]{:S(2)}, u32[]{:S(2)}) collective-permute-start(bf16[16,16,128]{2,1,0:T(8,128)(2,1)S(1)} %state.1), channel_id=1, source_target_pairs={{8,0},{16,8},{24,16},{9,1},{17,9},{25,17},{10,2},{18,10},{26,18},{... | collective-permute-start | bytes 196616 | tf_op jit(solution)/shard_map/ppermute | solution.py:443
  12.9 0.0 copy-done.9
  12.9 1.6 %table.1 = (bf16[2048,128]{1,0:T(8,128)(2,1)S(1)}, bf16[2048,128]{1,0:T(8,128)(2,1)S(1)}, bf16[2048,128]{1,0:T(8,128)(2,1)S(1)}, f32[128,128]{1,0:T(8,128)S(1)},...) custom-call(f32[16,128]{1,0:T(8,128)S(1)} %bitcast.34, f32[16,128]{1,0:T(8,128)S(1)} %bitcast.37), custom_call_target="tpu_custom_call" | custom-call | flops 1 | bytes 1 | tf_op jit(solution)/shard_map/table/pallas_call | solution.py:525
  14.5 2.3 %local.1 = f32[2048,128]{1,0:T(8,128)S(1)} custom-call(bf16[2048,128]{1,0:T(8,128)(2,1)S(1)} %bitcast.15, bf16[2048,128]{1,0:T(8,128)(2,1)S(1)} %bitcast.31, f32[128,128]{1,0:T(8,128)S(1)} %get-tuple-element.36.turned), custom_call_target="tpu_custom_call" | custom-call | flops 1 | bytes 1 | tf_op jit(solution)/shard_map/local/pallas_call | solution.py:529
  16.8 0.9 %collective-permute-done.2 = bf16[16,16,128]{2,1,0:T(8,128)(2,1)S(1)} collective-permute-done((bf16[16,16,128]{2,1,0:T(8,128)(2,1)S(1)}, bf16[16,16,128]{2,1,0:T(8,128)(2,1)S(1)}, u32[]{:S(2)}, u32[]{:S(2)}) %collective-permute-start.2) | collective-permute-done | bytes 65568 | tf_op jit(solution)/shard_map/ppermute | solution.py:443
  17.7 2.1 %collective-permute-done.1 = bf16[16,16,128]{2,1,0:T(8,128)(2,1)S(1)} collective-permute-done((bf16[16,16,128]{2,1,0:T(8,128)(2,1)S(1)}, bf16[16,16,128]{2,1,0:T(8,128)(2,1)S(1)}, u32[]{:S(2)}, u32[]{:S(2)}) %collective-permute-start.1) | collective-permute-done | bytes 65568 | tf_op jit(solution)/shard_map/ppermute | solution.py:443
  19.8 0.0 collective-permute-done
  19.8 0.1 add_multiply_fusion.states.after_shard
  19.8 0.0 collective-permute-done.3.before
  19.8 0.0 copy-done.1
  19.9 0.0 copy-start.6
  19.9 0.0 copy-start.8
  19.9 0.7 %middle.1 = (bf16[2048,128]{1,0:T(8,128)(2,1)S(1)}, f32[2048,128]{1,0:T(8,128)S(1)}) custom-call(f32[16,16,128]{2,1,0:T(8,128)S(1)} %add_multiply_fusion.states.after_shard, f32[2048,128]{1,0:T(8,128)S(1)} %local.1, bf16[2048,128]{1,0:T(8,128)(2,1)S(1)} %get-tuple-element.37.to_next, bf16[2048,128]{1,0:T(8,128)(2,1)S(1)} %bitcast.18, ...), custom_call_target="tpu_custom_call" | custom-call | flops 1 | bytes 1 | tf_op jit(solution)/shard_map/middle/pallas_call | solution.py:538
  20.6 1.3 %collective-permute-start.4 = (bf16[2048,128]{1,0:T(8,128)(2,1)S(1)}, bf16[2048,128]{1,0:T(8,128)(2,1)S(1)}, u32[]{:S(2)}, u32[]{:S(2)}) collective-permute-start(bf16[2048,128]{1,0:T(8,128)(2,1)S(1)} %get-tuple-element.38.dz1), channel_id=1, source_target_pairs={{8,0},{16,8},{24,16},{9,1},{17,9},{25,17},{10,2},{18,10},{26,18},{... | collective-permute-start | bytes 1572872 | tf_op jit(solution)/shard_map/ppermute | solution.py:443
  21.9 0.0 copy-done.6
  21.9 0.0 copy-done.8
  21.9 6.3 %forward.1 = (f32[2048,128]{1,0:T(8,128)S(1)}, bf16[2048,128]{1,0:T(8,128)(2,1)S(1)}, bf16[25,16,128]{2,1,0:T(8,128)(2,1)S(1)}) custom-call(bf16[2048,128]{1,0:T(8,128)(2,1)S(1)} %collective-permute-done.3.before, bf16[2048,128]{1,0:T(8,128)(2,1)S(1)} %copy-done.6, bf16[128,128]{1,0:T(8,128)(2,1)S(1)} %copy-done.8, bf16[2048,128]{1,0:T(8,128)(2,1)S(1)} %bitcast.22, ...), custom_call_target="tpu_custom_call" | custom-call | flops 1 | bytes 1 | tf_op jit(solution)/shard_map/forward/pallas_call | solution.py:547
  28.2 0.1 collective-permute-start.6
  28.3 5.7 %collective-permute-start.5 = (bf16[16,16,128]{2,1,0:T(8,128)(2,1)S(1)}, bf16[16,16,128]{2,1,0:T(8,128)(2,1)S(1)}, u32[]{:S(2)}, u32[]{:S(2)}) collective-permute-start(bf16[16,16,128]{2,1,0:T(8,128)(2,1)S(1)} %slice.12), channel_id=1, source_target_pairs={{0,16},{8,24},{1,17},{9,25},{2,18},{10,26},{3,19},{11,27},{4,20},{... | collective-permute-start | bytes 196616 | tf_op jit(solution)/shard_map/ppermute | solution.py:443
  34.1 3.1 %within.1 = (f32[2048,128]{1,0:T(8,128)S(1)}, bf16[2048,128]{1,0:T(8,128)(2,1)}, bf16[2048,128]{1,0:T(8,128)(2,1)}, f32[9,16,128]{2,1,0:T(8,128)S(1)}) custom-call(bf16[2048,128]{1,0:T(8,128)(2,1)S(1)} %get-tuple-element.46.u2, f32[128,128]{1,0:T(8,128)S(1)} %get-tuple-element.47.taps, f32[2048,128]{1,0:T(8,128)S(1)} %get-tuple-element.48.z1, ...), custom_call_target="tpu_custom_call" | custom-call | flops 1 | bytes 1 | tf_op jit(solution)/shard_map/within/pallas_call | solution.py:561
  37.2 0.0 collective-permute-done.6
  37.2 0.0 copy-start.3
  37.2 0.0 copy-start.4
  37.2 0.1 collective-permute-start.7
  37.3 0.0 collective-permute-done.4.later
  37.3 0.6 %factor.1 = (f32[9,16,128]{2,1,0:T(8,128)S(1)}, bf16[2048,128]{1,0:T(8,128)(2,1)S(1)}, f32[128,128]{1,0:T(8,128)S(1)}, f32[16,16,128]{2,1,0:T(8,128)S(1)}, f32[16,16,128]{2,1,0:T(8,128)S(1)}) custom-call(f32[16,16,128]{2,1,0:T(8,128)S(1)} %get-tuple-element.35.wide_rate, f32[16,128]{1,0:T(8,128)S(1)} %bitcast.36, f32[16,128]{1,0:T(8,128)S(1)} %bitcast.38, ...), custom_call_target="tpu_custom_call" | custom-call | flops 1 | bytes 1 | tf_op jit(solution)/shard_map/factor/pallas_call | solution.py:568
  38.0 0.0 collective-permute-done.5
  38.0 0.2 copy-done.3
  38.3 0.2 copy-done.4
  38.4 2.0 %product.2 = (bf16[2048,128]{1,0:T(8,128)(2,1)}, bf16[2048,128]{1,0:T(8,128)(2,1)}, f32[9,16,128]{2,1,0:T(8,128)S(1)}) custom-call(bf16[2048,128]{1,0:T(8,128)(2,1)S(1)} %get-tuple-element.38.dz1, bf16[2048,128]{1,0:T(8,128)(2,1)S(1)} %collective-permute-done.4.later, f32[128,128]{1,0:T(8,128)S(1)} %get-tuple-element.39.turned, ...), custom_call_target="tpu_custom_call" | custom-call | flops 1 | bytes 1 | tf_op jit(solution)/shard_map/product/pallas_call | solution.py:580
  40.4 2.1 %collective-permute-done.7 = bf16[9,16,128]{2,1,0:T(8,128)(2,1)S(1)} collective-permute-done((bf16[9,16,128]{2,1,0:T(8,128)(2,1)S(1)}, bf16[9,16,128]{2,1,0:T(8,128)(2,1)S(1)}, u32[]{:S(2)}, u32[]{:S(2)}) %collective-permute-start.7) | collective-permute-done | bytes 36896 | tf_op jit(solution)/shard_map/ppermute | solution.py:448
  42.6 1.3 %collective-permute-start.8 = (bf16[25,16,128]{2,1,0:T(8,128)(2,1)S(1)}, bf16[25,16,128]{2,1,0:T(8,128)(2,1)S(1)}, u32[]{:S(2)}, u32[]{:S(2)}) collective-permute-start(bf16[25,16,128]{2,1,0:T(8,128)(2,1)S(1)} %pad_maximum_fusion), channel_id=1, source_target_pairs={{0,8},{8,0},{16,24},{24,16},{1,9},{9,1},{17,25},{25,17},{2,10},{10... | collective-permute-start | bytes 307208 | tf_op jit(solution)/shard_map/ppermute | solution.py:448
  43.9 2.0 %product.3 = (bf16[2048,128]{1,0:T(8,128)(2,1)}, bf16[2048,128]{1,0:T(8,128)(2,1)}) custom-call(bf16[2048,128]{1,0:T(8,128)(2,1)S(1)} %get-tuple-element.38.dz1, bf16[2048,128]{1,0:T(8,128)(2,1)S(1)} %collective-permute-done.4.later, f32[128,128]{1,0:T(8,128)S(1)} %get-tuple-element.39.turned, ...), custom_call_target="tpu_custom_call", output_to_operand_aliasing={{0}: (5, {}), {1}: (6, {})} | custom-call | flops 1 | bytes 1 | tf_op jit(solution)/shard_map/product/pallas_call | solution.py:580
  45.9 1.4 %collective-permute-done.8 = bf16[25,16,128]{2,1,0:T(8,128)(2,1)S(1)} collective-permute-done((bf16[25,16,128]{2,1,0:T(8,128)(2,1)S(1)}, bf16[25,16,128]{2,1,0:T(8,128)(2,1)S(1)}, u32[]{:S(2)}, u32[]{:S(2)}) %collective-permute-start.8) | collective-permute-done | bytes 102432 | tf_op jit(solution)/shard_map/ppermute | solution.py:448
  47.3 0.1 fusion.3.states
  47.4 1.8 %value.1 = (bf16[2048,128]{1,0:T(8,128)(2,1)}, f32[128,128]{1,0:T(8,128)}, f32[16,128]{1,0:T(8,128)}) custom-call(f32[16,16,128]{2,1,0:T(8,128)S(1)} %fusion.3.states, bf16[2048,128]{1,0:T(8,128)(2,1)S(1)} %get-tuple-element.58.after, f32[2048,128]{1,0:T(8,128)S(1)} %get-tuple-element.59.z2, bf16[2048,128]{1,0:T(8,128)(2,1)S(1)} %bitcast.17, ...), custom_call_target="tpu_custom_call" | custom-call | flops 1 | bytes 1 | tf_op jit(solution)/shard_map/value/pallas_call | solution.py:607
  (10 shorter events, 0.1 us)
Async XLA Ops:
  0.6 7.2 %copy-start = (bf16[1,2048,128]{2,1,0:T(8,128)(2,1)S(1)}, bf16[1,2048,128]{2,1,0:T(8,128)(2,1)}, u32[]{:S(2)}) copy-start(bf16[1,2048,128]{2,1,0:T(8,128)(2,1)} %param.14) | copy-start | bytes 1572868
  0.6 7.2 %copy-start.5 = (bf16[1,2048,128]{2,1,0:T(8,128)(2,1)S(1)}, bf16[1,2048,128]{2,1,0:T(8,128)(2,1)}, u32[]{:S(2)}) copy-start(bf16[1,2048,128]{2,1,0:T(8,128)(2,1)} %param.13) | copy-start | bytes 1572868
  0.7 7.2 %copy-start.7 = (f32[128,16]{0,1:T(8,128)S(1)}, f32[128,16]{0,1:T(8,128)}, u32[]{:S(2)}) copy-start(f32[128,16]{0,1:T(8,128)} %param.17) | copy-start | bytes 24580
  2.8 17.0 %collective-permute-start.3 = (bf16[2048,128]{1,0:T(8,128)(2,1)}, bf16[2048,128]{1,0:T(8,128)(2,1)S(1)}, u32[]{:S(2)}, u32[]{:S(2)}) collective-permute-start(bf16[2048,128]{1,0:T(8,128)(2,1)} %gate.1.now), channel_id=1, source_target_pairs={{0,8},{8,16},{16,24},{1,9},{9,17},{17,25},{2,10},{10,18},{18,26},{... | collective-permute-start | bytes 1572872 | tf_op jit(solution)/shard_map/ppermute | solution.py:443
  7.8 5.1 %copy-start.9 = (f32[128,16]{0,1:T(8,128)S(1)}, f32[128,16]{0,1:T(8,128)}, u32[]{:S(2)}) copy-start(f32[128,16]{0,1:T(8,128)} %param.16) | copy-start | bytes 24580
  9.0 8.7 %collective-permute-start.2 = (bf16[16,16,128]{2,1,0:T(8,128)(2,1)S(1)}, bf16[16,16,128]{2,1,0:T(8,128)(2,1)S(1)}, u32[]{:S(2)}, u32[]{:S(2)}) collective-permute-start(bf16[16,16,128]{2,1,0:T(8,128)(2,1)S(1)} %state.1), channel_id=1, source_target_pairs={{24,0},{25,1},{26,2},{27,3},{28,4},{29,5},{30,6},{31,7}} | collective-permute-start | bytes 196616 | tf_op jit(solution)/shard_map/ppermute | solution.py:443
  10.3 9.4 %collective-permute-start.1 = (bf16[16,16,128]{2,1,0:T(8,128)(2,1)S(1)}, bf16[16,16,128]{2,1,0:T(8,128)(2,1)S(1)}, u32[]{:S(2)}, u32[]{:S(2)}) collective-permute-start(bf16[16,16,128]{2,1,0:T(8,128)(2,1)S(1)} %state.1), channel_id=1, source_target_pairs={{16,0},{24,8},{17,1},{25,9},{18,2},{26,10},{19,3},{27,11},{20,4},{... | collective-permute-start | bytes 196616 | tf_op jit(solution)/shard_map/ppermute | solution.py:443
  11.6 8.2 %collective-permute-start = (bf16[16,16,128]{2,1,0:T(8,128)(2,1)S(1)}, bf16[16,16,128]{2,1,0:T(8,128)(2,1)S(1)}, u32[]{:S(2)}, u32[]{:S(2)}) collective-permute-start(bf16[16,16,128]{2,1,0:T(8,128)(2,1)S(1)} %state.1), channel_id=1, source_target_pairs={{8,0},{16,8},{24,16},{9,1},{17,9},{25,17},{10,2},{18,10},{26,18},{... | collective-permute-start | bytes 196616 | tf_op jit(solution)/shard_map/ppermute | solution.py:443
  14.5 5.4 %copy-start.1 = (bf16[1,2048,128]{2,1,0:T(8,128)(2,1)S(1)}, bf16[1,2048,128]{2,1,0:T(8,128)(2,1)}, u32[]{:S(2)}) copy-start(bf16[1,2048,128]{2,1,0:T(8,128)(2,1)} %param.12) | copy-start | bytes 1572868
  14.5 5.4 %copy-start.2 = (bf16[1,2048,128]{2,1,0:T(8,128)(2,1)S(1)}, bf16[1,2048,128]{2,1,0:T(8,128)(2,1)}, u32[]{:S(2)}) copy-start(bf16[1,2048,128]{2,1,0:T(8,128)(2,1)} %param.11) | copy-start | bytes 1572868
  19.9 2.0 %copy-start.6 = (bf16[2048,128]{1,0:T(8,128)(2,1)S(1)}, bf16[2048,128]{1,0:T(8,128)(2,1)}, u32[]{:S(2)}) copy-start(bf16[2048,128]{1,0:T(8,128)(2,1)} %gate.1.now) | copy-start | bytes 1572868
  19.9 2.0 %copy-start.8 = (bf16[128,128]{1,0:T(8,128)(2,1)S(1)}, bf16[128,128]{1,0:T(8,128)(2,1)}, u32[]{:S(2)}) copy-start(bf16[128,128]{1,0:T(8,128)(2,1)} %filters.3) | copy-start | bytes 98308
  20.6 16.7 %collective-permute-start.4 = (bf16[2048,128]{1,0:T(8,128)(2,1)S(1)}, bf16[2048,128]{1,0:T(8,128)(2,1)S(1)}, u32[]{:S(2)}, u32[]{:S(2)}) collective-permute-start(bf16[2048,128]{1,0:T(8,128)(2,1)S(1)} %get-tuple-element.38.dz1), channel_id=1, source_target_pairs={{8,0},{16,8},{24,16},{9,1},{17,9},{25,17},{10,2},{18,10},{26,18},{... | collective-permute-start | bytes 1572872 | tf_op jit(solution)/shard_map/ppermute | solution.py:443
  28.2 8.9 %collective-permute-start.6 = (bf16[9,16,128]{2,1,0:T(8,128)(2,1)S(1)}, bf16[9,16,128]{2,1,0:T(8,128)(2,1)S(1)}, u32[]{:S(2)}, u32[]{:S(2)}) collective-permute-start(bf16[9,16,128]{2,1,0:T(8,128)(2,1)S(1)} %slice.13), channel_id=1, source_target_pairs={{0,1},{1,0},{2,3},{3,2},{4,5},{5,4},{6,7},{7,6},{8,9},{9,8},{10,11... | collective-permute-start | bytes 110600 | tf_op jit(solution)/shard_map/ppermute | solution.py:448
  28.3 9.6 %collective-permute-start.5 = (bf16[16,16,128]{2,1,0:T(8,128)(2,1)S(1)}, bf16[16,16,128]{2,1,0:T(8,128)(2,1)S(1)}, u32[]{:S(2)}, u32[]{:S(2)}) collective-permute-start(bf16[16,16,128]{2,1,0:T(8,128)(2,1)S(1)} %slice.12), channel_id=1, source_target_pairs={{0,16},{8,24},{1,17},{9,25},{2,18},{10,26},{3,19},{11,27},{4,20},{... | collective-permute-start | bytes 196616 | tf_op jit(solution)/shard_map/ppermute | solution.py:443
  37.2 1.0 %copy-start.3 = (bf16[1,2048,128]{2,1,0:T(8,128)(2,1)S(1)}, bf16[1,2048,128]{2,1,0:T(8,128)(2,1)}, u32[]{:S(2)}) copy-start(bf16[1,2048,128]{2,1,0:T(8,128)(2,1)} %param.9) | copy-start | bytes 1572868
  37.2 1.2 %copy-start.4 = (bf16[1,2048,128]{2,1,0:T(8,128)(2,1)S(1)}, bf16[1,2048,128]{2,1,0:T(8,128)(2,1)}, u32[]{:S(2)}) copy-start(bf16[1,2048,128]{2,1,0:T(8,128)(2,1)} %param.10) | copy-start | bytes 1572868
  37.2 5.3 %collective-permute-start.7 = (bf16[9,16,128]{2,1,0:T(8,128)(2,1)S(1)}, bf16[9,16,128]{2,1,0:T(8,128)(2,1)S(1)}, u32[]{:S(2)}, u32[]{:S(2)}) collective-permute-start(bf16[9,16,128]{2,1,0:T(8,128)(2,1)S(1)} %add_convert_fusion.1), channel_id=1, source_target_pairs={{0,16},{8,24},{16,0},{24,8},{1,17},{9,25},{17,1},{25,9},{2,18},{10... | collective-permute-start | bytes 110600 | tf_op jit(solution)/shard_map/ppermute | solution.py:448
  42.6 4.7 %collective-permute-start.8 = (bf16[25,16,128]{2,1,0:T(8,128)(2,1)S(1)}, bf16[25,16,128]{2,1,0:T(8,128)(2,1)S(1)}, u32[]{:S(2)}, u32[]{:S(2)}) collective-permute-start(bf16[25,16,128]{2,1,0:T(8,128)(2,1)S(1)} %pad_maximum_fusion), channel_id=1, source_target_pairs={{0,8},{8,0},{16,24},{24,16},{1,9},{9,1},{17,25},{25,17},{2,10},{10... | collective-permute-start | bytes 307208 | tf_op jit(solution)/shard_map/ppermute | solution.py:448
